TPU v7x, 32 devices: a whole 2x2x4 slice. The times are simulated.
32 devices in a mesh: gx: 8 (over y, x, core), gy: 4 (over z).
Axes of the slice: x: 2, y: 2, z: 4, core: 2. Of those that a mesh axis runs over, the one named last changes fastest.
Arguments:
- modes: float32 [4, 32, 2048], P(None, 'gx', 'gy'), may hold values from -6 to 6
- directions: float32 [4, 32, 2048], P(None, 'gx', 'gy'), may hold values from -6 to 6
- locked: float32 [60, 32, 2048], P(None, 'gx', 'gy'), may hold values from -9 to 9
- perm_class: int32 [32, 2048], P('gx', 'gy'), may hold values from 0 to 15
- perm_table: float32 [16], replicated, may hold values from 0.01 to 1
- locked_count: int32 [1], replicated, may hold values from 30 to 60
Outputs:
- new_modes: float32 [4, 32, 2048], P(None, 'gx', 'gy')
- new_directions: float32 [4, 32, 2048], P(None, 'gx', 'gy')
- ritz_values: float32 [4], replicated
- locked_correlation: float32 [60, 4], replicated
All inputs are finite; a program needn't handle non-finite values.
Results may differ from a plain program's by a relative error of at most 0.0003.
Values sent between devices are 32-bit elements; how exact they have to be, the bound alone decides.
A program may use at most 64 MiB of HBM per device.

v0:
```python
import jax
import jax.numpy as jnp
from jax import lax
from jax.sharding import PartitionSpec as P

NZ = 64
ACTIVE = 4
SWEEPS = 3
RITZ = 3


OMEGA = 0.6
EPSILON = 1e-06
PRECISE = lax.Precision.HIGHEST


def extended(block, sides, width):
    for axis, dim in sides:
        count = lax.axis_size(axis)
        forward = [(i, i + 1) for i in range(count - 1)]
        backward = [(target, source) for source, target in forward]
        low = lax.ppermute(
            lax.slice_in_dim(block, block.shape[dim] - width, None, axis=dim), axis, forward
        )
        high = lax.ppermute(lax.slice_in_dim(block, 0, width, axis=dim), axis, backward)
        block = jnp.concatenate([low, block, high], axis=dim)
    return block


def face_value(lower_k, upper_k):
    return jnp.where(
        lower_k > 0,
        jnp.where(upper_k > 0, 2.0 * lower_k * upper_k / (lower_k + upper_k), 2.0 * lower_k),
        2.0 * upper_k,
    )


def assemble(x_lower, x_upper, y_lower, y_upper, z_lower, z_upper):
    diagonal = x_lower + x_upper + y_lower + y_upper + z_lower + z_upper
    return jnp.stack([diagonal, x_lower, x_upper, y_lower, y_upper, z_lower, z_upper])


def fine_coef(rimmed):
    interior = rimmed[1:-1, 1:-1]
    z_padded = jnp.pad(interior, ((0, 0), (0, 0), (1, 1)))
    x_lower = face_value(rimmed[:-2, 1:-1], interior)
    x_upper = face_value(interior, rimmed[2:, 1:-1])
    y_lower = face_value(rimmed[1:-1, :-2], interior)
    y_upper = face_value(interior, rimmed[1:-1, 2:])
    z_lower = face_value(z_padded[:, :, :-2], interior)
    z_upper = face_value(interior, z_padded[:, :, 2:])
    return assemble(x_lower, x_upper, y_lower, y_upper, z_lower, z_upper)


def pair_sum(blocks, which_dim):
    extent = blocks.shape
    return blocks.reshape(
        extent[:which_dim] + (extent[which_dim] // 2, 2) + extent[which_dim + 1 :]
    ).sum(which_dim + 1)


def coarsen(coeffs):
    x_lower = pair_sum(pair_sum(coeffs[1][0::2], 1), 2)
    x_upper = pair_sum(pair_sum(coeffs[2][1::2], 1), 2)
    y_lower = pair_sum(pair_sum(coeffs[3][:, 0::2], 0), 2)
    y_upper = pair_sum(pair_sum(coeffs[4][:, 1::2], 0), 2)
    z_lower = pair_sum(pair_sum(coeffs[5][:, :, 0::2], 0), 1)
    z_upper = pair_sum(pair_sum(coeffs[6][:, :, 1::2], 0), 1)
    return assemble(x_lower, x_upper, y_lower, y_upper, z_lower, z_upper)


def stencil(rimmed, coeffs):
    center = rimmed[:, 1:-1, 1:-1]
    z_padded = jnp.pad(center, ((0, 0), (0, 0), (0, 0), (1, 1)))
    beside = coeffs[1] * rimmed[:, :-2, 1:-1] + coeffs[2] * rimmed[:, 2:, 1:-1]
    beside = beside + coeffs[3] * rimmed[:, 1:-1, :-2] + coeffs[4] * rimmed[:, 1:-1, 2:]
    beside = beside + coeffs[5] * z_padded[..., :-2] + coeffs[6] * z_padded[..., 2:]
    return coeffs[0] * center - beside


def restrict(field):
    return pair_sum(pair_sum(pair_sum(field, 1), 2), 3)


def prolong(field):
    return jnp.repeat(jnp.repeat(jnp.repeat(field, 2, 1), 2, 2), 2, 3)


def line_solve(source, coeffs, shift):
    lower = jnp.transpose(coeffs[3], (0, 2, 1))
    upper = jnp.transpose(coeffs[4], (0, 2, 1))
    others = jnp.transpose(coeffs[1] + coeffs[2] + coeffs[5] + coeffs[6], (0, 2, 1))
    main = lower + upper + shift * others
    below = jnp.concatenate([jnp.zeros_like(lower[..., :1]), -lower[..., 1:]], -1)
    above = jnp.concatenate([-upper[..., :-1], jnp.zeros_like(upper[..., :1])], -1)
    right = jnp.transpose(source, (1, 3, 2, 0))
    solved = lax.linalg.tridiagonal_solve(below, main, above, right)
    return jnp.transpose(solved, (3, 0, 2, 1))


def fine_apply(field, coeffs):
    return stencil(extended(field, (("gx", 1), ("gy", 2)), 1), coeffs)


def middle_apply(field, coeffs):
    return stencil(extended(field, (("gx", 1), ("gy", 2)), 1), coeffs)


def coarse_solve(source, coeffs):
    span_coarse = source.shape[2]
    gathered = lax.all_gather(source, "gy", axis=2, tiled=True)
    line_len = gathered.shape[2]
    update = line_solve(gathered, coeffs, 4.0 / float(line_len * line_len))
    for sweep_no in range(SWEEPS - 1):
        rimmed = extended(update, (("gx", 1),), 1)
        rimmed = jnp.pad(rimmed, ((0, 0), (0, 0), (1, 1), (0, 0)))
        update = update + OMEGA * (gathered - stencil(rimmed, coeffs)) / coeffs[0]
    return lax.dynamic_slice_in_dim(update, lax.axis_index("gy") * span_coarse, span_coarse, 2)


def vcycle(residual, fine_coeffs, middle_coeffs, coarse_coeffs):
    error_fine = OMEGA * residual / fine_coeffs[0]
    source_mid = restrict(residual - fine_apply(error_fine, fine_coeffs))
    error_mid = OMEGA * source_mid / middle_coeffs[0]
    source_low = restrict(source_mid - middle_apply(error_mid, middle_coeffs))
    error_low = coarse_solve(source_low, coarse_coeffs)
    error_mid = error_mid + prolong(error_low)
    error_mid = (
        error_mid + OMEGA * (source_mid - middle_apply(error_mid, middle_coeffs)) / middle_coeffs[0]
    )
    error_fine = error_fine + prolong(error_mid)
    return error_fine + OMEGA * (residual - fine_apply(error_fine, fine_coeffs)) / fine_coeffs[0]


def rayleigh_ritz(gram_m, gram_a):
    gram_a = 0.5 * (gram_a + gram_a.T)
    chol_m = jnp.linalg.cholesky(gram_m)
    half_solved = lax.linalg.triangular_solve(chol_m, gram_a, left_side=True, lower=True)
    reduced = lax.linalg.triangular_solve(chol_m, half_solved.T, left_side=True, lower=True)
    reduced = 0.5 * (reduced + reduced.T)
    spectral_top = jnp.trace(reduced)
    basis_q = jnp.eye(gram_m.shape[0], ACTIVE, dtype=jnp.float32)
    for ritz_step in range(RITZ):
        raised = spectral_top * basis_q - jnp.dot(reduced, basis_q, precision=PRECISE)
        factor = jnp.linalg.cholesky(jnp.dot(raised.T, raised, precision=PRECISE))
        basis_q = lax.linalg.triangular_solve(factor, raised.T, left_side=True, lower=True).T
    ritz_values = jnp.sum(basis_q * jnp.dot(reduced, basis_q, precision=PRECISE), axis=0)
    coefficients = lax.linalg.triangular_solve(
        chol_m, basis_q, left_side=True, lower=True, transpose_a=True
    )
    return (coefficients, ritz_values)


def on_device(modes, directions, locked, perm_class, perm_table, locked_count):
    active, rows_dev, plane_dev = modes.shape
    z_cells = NZ
    span_dev = plane_dev // z_cells
    classes = jnp.arange(perm_table.shape[0], dtype=jnp.int32)
    conduct = jnp.sum(
        jnp.where(perm_class[None] == classes[:, None, None], perm_table[:, None, None], 0.0),
        axis=0,
    )
    conduct = conduct.reshape(rows_dev, span_dev, z_cells)
    rimmed = extended(conduct, (("gx", 0), ("gy", 1)), 1)
    fine_coeffs = fine_coef(rimmed)
    middle_coeffs = coarsen(fine_coeffs)
    coarse_coeffs = coarsen(middle_coeffs)
    coarse_coeffs = lax.all_gather(coarse_coeffs, "gy", axis=2, tiled=True)
    field_x = modes.reshape(active, rows_dev, span_dev, z_cells)
    field_p = directions.reshape(active, rows_dev, span_dev, z_cells)
    locked_grid = locked.reshape(locked.shape[0], rows_dev, span_dev, z_cells)
    cell_count = float(rows_dev * span_dev * z_cells * lax.axis_size("gx") * lax.axis_size("gy"))
    start_fields = jnp.concatenate([field_x, field_p], 0)
    start_images = stencil(extended(start_fields, (("gx", 1), ("gy", 2)), 1), fine_coeffs)
    image_x = start_images[:active]
    image_p = start_images[active:]
    top_part = jnp.einsum("kxyz,kxyz->k", field_x, image_x, precision=PRECISE)
    norm_part = jnp.einsum("kxyz,kxyz->k", field_x, field_x, precision=PRECISE)
    in_use = (jnp.arange(locked.shape[0], dtype=jnp.int32) < locked_count[0])[:, None]
    image_part = jnp.einsum("jxyz,kxyz->jk", locked_grid, image_x, precision=PRECISE)
    mode_part = jnp.einsum("jxyz,kxyz->jk", locked_grid, field_x, precision=PRECISE)
    top_sum, norm_sum, image_sum, mode_sum = lax.psum(
        (top_part, norm_part, image_part, mode_part), ("gx", "gy")
    )
    rayleigh_q = top_sum / cell_count / (norm_sum / cell_count + EPSILON)
    residual = image_x - rayleigh_q[:, None, None, None] * field_x
    coupling = image_sum / cell_count - mode_sum / cell_count * rayleigh_q[None, :]
    coupling = jnp.where(in_use, coupling, 0.0)
    residual = residual - jnp.einsum("jk,jxyz->kxyz", coupling, locked_grid, precision=PRECISE)
    precond = vcycle(residual, fine_coeffs, middle_coeffs, coarse_coeffs)
    correlation_part = jnp.einsum("jxyz,kxyz->jk", locked_grid, precond, precision=PRECISE)
    correlation = jnp.where(in_use, lax.psum(correlation_part, ("gx", "gy")) / cell_count, 0.0)
    projected = precond - jnp.einsum("jk,jxyz->kxyz", correlation, locked_grid, precision=PRECISE)
    image_w = fine_apply(projected, fine_coeffs)
    trial = jnp.concatenate([field_x, projected, field_p], 0)
    images = jnp.concatenate([image_x, image_w, image_p], 0)
    mass_part = jnp.einsum("axyz,bxyz->ab", trial, trial, precision=PRECISE)
    stiff_part = jnp.einsum("axyz,bxyz->ab", trial, images, precision=PRECISE)
    mass_sum, stiff_sum = lax.psum((mass_part, stiff_part), ("gx", "gy"))
    coefficients, ritz_values = rayleigh_ritz(mass_sum / cell_count, stiff_sum / cell_count)
    new_modes = jnp.einsum("ak,axyz->kxyz", coefficients, trial, precision=PRECISE)
    new_directions = jnp.einsum(
        "ak,axyz->kxyz", coefficients[active:], trial[active:], precision=PRECISE
    )
    return (
        new_modes.reshape(active, rows_dev, plane_dev),
        new_directions.reshape(active, rows_dev, plane_dev),
        ritz_values,
        correlation,
    )


def solution(mesh):
    placed = (
        P(None, "gx", "gy"),
        P(None, "gx", "gy"),
        P(None, "gx", "gy"),
        P("gx", "gy"),
        P(),
        P(),
    )
    return jax.shard_map(
        on_device,
        mesh=mesh,
        in_specs=placed,
        out_specs=(P(None, "gx", "gy"), P(None, "gx", "gy"), P(), P()),
        check_vma=False,
    )
```

profile of v0, /device:TPU:0, one launch (start us, length us, event | category | flops | bytes accessed | tf_op | source)
XLA Modules:
  0.0 314.6 jit_solution(12104347302247162762)
XLA Ops:
  1.6 2.3 collective-permute-start
  7.7 5.8 %collective-permute-start.4 = (f32[8,1,8,64]{3,0,2,1:T(8,128)S(1)}, f32[8,1,8,64]{3,0,2,1:T(8,128)S(1)}, u32[]{:S(2)}, u32[]{:S(2)}) collective-permute-start(f32[8,1,8,64]{3,0,2,1:T(8,128)S(1)} %get-tuple-element.60), channel_id=1, source_target_pairs={{0,4},{4,8},{8,12},{12,16},{16,20},{20,24},{24,28},{1,5},{5,9},{9,... | collective-permute-start | bytes 49160 | tf_op jit(solution)/shard_map/ppermute | solution.py:22
  15.0 3.5 %collective-permute-start.2 = (f32[6,1,64]{2,1,0:T(1,128)S(1)}, f32[6,1,64]{2,1,0:T(1,128)S(1)}, u32[]{:S(2)}, u32[]{:S(2)}) collective-permute-start(f32[6,1,64]{2,1,0:T(1,128)S(1)} %get-tuple-element.82), channel_id=1, source_target_pairs={{0,1},{1,2},{2,3},{4,5},{5,6},{6,7},{8,9},{9,10},{10,11},{12,13},{... | collective-permute-start | bytes 4616 | tf_op jit(solution)/shard_map/ppermute | solution.py:22
  18.5 1.3 collective-permute-start.3
  20.2 3.8 %collective-permute-done.3 = f32[6,1,64]{2,1,0:T(1,128)S(1)} collective-permute-done((f32[6,1,64]{2,1,0:T(1,128)S(1)}, f32[6,1,64]{2,1,0:T(1,128)S(1)}, u32[]{:S(2)}, u32[]{:S(2)}) %collective-permute-start.3) | collective-permute-done | bytes 1568 | tf_op jit(solution)/shard_map/ppermute | solution.py:25
  27.1 13.4 %all_gather.7 = f32[7,1,8,16]{3,1,0,2:T(1,128)S(1)} all-gather(f32[7,1,2,16]{3,1,0,2:T(1,128)S(1)} %copy.487), channel_id=1, replica_groups=mesh['gx'=8,'gy'=4] {'gy'}, dimensions={2}, use_global_device_ids=true | all-gather | bytes 4480 | tf_op jit(solution)/shard_map/all_gather | solution.py:168
  40.6 1.3 collective-permute-start.7
  41.9 4.5 %collective-permute-start.6 = (f32[8,6,1,64]{3,0,2,1:T(8,128)S(1)}, f32[8,6,1,64]{3,0,2,1:T(8,128)S(1)}, u32[]{:S(2)}, u32[]{:S(2)}) collective-permute-start(f32[8,6,1,64]{3,0,2,1:T(8,128)S(1)} %get-tuple-element.52), channel_id=1, source_target_pairs={{0,1},{1,2},{2,3},{4,5},{5,6},{6,7},{8,9},{9,10},{10,11},{12,13},{... | collective-permute-start | bytes 36872 | tf_op jit(solution)/shard_map/ppermute | solution.py:22
  46.5 1.5 collective-permute-done.6
  48.2 1.3 convolution_bitcast_fusion.5
  49.6 41.7 %all-reduce.13 = (f32[4]{0:T(128)S(1)}, f32[4]{0:T(128)S(1)}, f32[60,4]{0,1:T(4,128)S(1)}, f32[60,4]{0,1:T(4,128)S(1)}) all-reduce(f32[4]{0:T(128)S(1)} %get-tuple-element.8, f32[4]{0:T(128)S(1)} %get-tuple-element.7, f32[60,4]{0,1:T(4,128)S(1)} %convolution_bitcast_fusion.3, ...), channel_id=1, replica_groups=mesh['gx'=8,'gy'=4] {'gx','gy'}, use_global_device_ids=true, to_apply=%region_2.3 | all-reduce | flops 488 | bytes 3904 | tf_op jit(solution)/shard_map/psum | solution.py:182
  93.8 3.0 collective-permute-start.8
  98.9 4.5 %collective-permute-start.10 = (f32[4,6,1,64]{3,0,2,1:T(4,128)S(1)}, f32[4,6,1,64]{3,0,2,1:T(4,128)S(1)}, u32[]{:S(2)}, u32[]{:S(2)}) collective-permute-start(f32[4,6,1,64]{3,0,2,1:T(4,128)S(1)} %get-tuple-element.66), channel_id=1, source_target_pairs={{0,1},{1,2},{2,3},{4,5},{5,6},{6,7},{8,9},{9,10},{10,11},{12,13},{... | collective-permute-start | bytes 18440 | tf_op jit(solution)/shard_map/ppermute | solution.py:22
  103.6 1.3 collective-permute-done.10
  106.9 3.3 %collective-permute-start.12 = (f32[4,1,4,32]{2,3,1,0:T(8,128)S(1)}, f32[4,1,4,32]{2,3,1,0:T(8,128)S(1)}, u32[]{:S(2)}, u32[]{:S(2)}) collective-permute-start(f32[4,1,4,32]{2,3,1,0:T(8,128)S(1)} %get-tuple-element.58), channel_id=1, source_target_pairs={{0,4},{4,8},{8,12},{12,16},{16,20},{20,24},{24,28},{1,5},{5,9},{9,... | collective-permute-start | bytes 6152 | tf_op jit(solution)/shard_map/ppermute | solution.py:22
  112.6 4.6 %collective-permute-start.14 = (f32[4,4,1,32]{2,3,1,0:T(8,128)S(1)}, f32[4,4,1,32]{2,3,1,0:T(8,128)S(1)}, u32[]{:S(2)}, u32[]{:S(2)}) collective-permute-start(f32[4,4,1,32]{2,3,1,0:T(8,128)S(1)} %get-tuple-element.50), channel_id=1, source_target_pairs={{0,1},{1,2},{2,3},{4,5},{5,6},{6,7},{8,9},{9,10},{10,11},{12,13},{... | collective-permute-start | bytes 6152 | tf_op jit(solution)/shard_map/ppermute | solution.py:22
  117.2 2.4 collective-permute-done.15
  119.5 1.5 collective-permute-done.14
  121.6 14.7 %all-gather = f32[4,8,16]{2,0,1:T(4,128)S(1)} all-gather(f32[4,2,16]{2,0,1:T(4,128)S(1)} %copy.478), channel_id=2, replica_groups=mesh['gx'=8,'gy'=4] {'gy'}, dimensions={1}, use_global_device_ids=true | all-gather | bytes 2560 | tf_op jit(solution)/shard_map/all_gather | solution.py:111
  137.7 3.0 collective-permute-start.16
  143.0 10.3 %collective-permute-start.18 = (f32[4,1,8,16]{3,0,2,1:T(4,128)S(1)}, f32[4,1,8,16]{3,0,2,1:T(4,128)S(1)}, u32[]{:S(2)}, u32[]{:S(2)}) collective-permute-start(f32[4,1,8,16]{3,0,2,1:T(4,128)S(1)} %divide_add_fusion.1), channel_id=1, source_target_pairs={{0,4},{4,8},{8,12},{12,16},{16,20},{20,24},{24,28},{1,5},{5,9},{9,... | collective-permute-start | bytes 6152 | tf_op jit(solution)/shard_map/ppermute | solution.py:22
  155.8 4.9 %collective-permute-start.20 = (f32[4,1,4,32]{2,3,1,0:T(8,128)S(1)}, f32[4,1,4,32]{2,3,1,0:T(8,128)S(1)}, u32[]{:S(2)}, u32[]{:S(2)}) collective-permute-start(f32[4,1,4,32]{2,3,1,0:T(8,128)S(1)} %get-tuple-element.56), channel_id=1, source_target_pairs={{0,4},{4,8},{8,12},{12,16},{16,20},{20,24},{24,28},{1,5},{5,9},{9,... | collective-permute-start | bytes 6152 | tf_op jit(solution)/shard_map/ppermute | solution.py:22
  163.0 4.6 %collective-permute-start.22 = (f32[4,4,1,32]{2,3,1,0:T(8,128)S(1)}, f32[4,4,1,32]{2,3,1,0:T(8,128)S(1)}, u32[]{:S(2)}, u32[]{:S(2)}) collective-permute-start(f32[4,4,1,32]{2,3,1,0:T(8,128)S(1)} %get-tuple-element.48), channel_id=1, source_target_pairs={{0,1},{1,2},{2,3},{4,5},{5,6},{6,7},{8,9},{9,10},{10,11},{12,13},{... | collective-permute-start | bytes 6152 | tf_op jit(solution)/shard_map/ppermute | solution.py:22
  167.6 3.4 %collective-permute-done.23 = f32[4,4,1,32]{2,3,1,0:T(8,128)S(1)} collective-permute-done((f32[4,4,1,32]{2,3,1,0:T(8,128)S(1)}, f32[4,4,1,32]{2,3,1,0:T(8,128)S(1)}, u32[]{:S(2)}, u32[]{:S(2)}) %collective-permute-start.23) | collective-permute-done | bytes 2080 | tf_op jit(solution)/shard_map/ppermute | solution.py:25
  171.0 1.7 collective-permute-done.22
  174.9 4.2 %collective-permute-start.24 = (f32[4,1,8,64]{3,0,2,1:T(4,128)S(1)}, f32[4,1,8,64]{3,0,2,1:T(4,128)S(1)}, u32[]{:S(2)}, u32[]{:S(2)}) collective-permute-start(f32[4,1,8,64]{3,0,2,1:T(4,128)S(1)} %get-tuple-element.70), channel_id=1, source_target_pairs={{0,4},{4,8},{8,12},{12,16},{16,20},{20,24},{24,28},{1,5},{5,9},{9,... | collective-permute-start | bytes 24584 | tf_op jit(solution)/shard_map/ppermute | solution.py:22
  181.2 4.9 %collective-permute-start.26 = (f32[4,6,1,64]{3,0,2,1:T(4,128)S(1)}, f32[4,6,1,64]{3,0,2,1:T(4,128)S(1)}, u32[]{:S(2)}, u32[]{:S(2)}) collective-permute-start(f32[4,6,1,64]{3,0,2,1:T(4,128)S(1)} %get-tuple-element.64), channel_id=1, source_target_pairs={{0,1},{1,2},{2,3},{4,5},{5,6},{6,7},{8,9},{9,10},{10,11},{12,13},{... | collective-permute-start | bytes 18440 | tf_op jit(solution)/shard_map/ppermute | solution.py:22
  187.4 1.4 convolution_bitcast_fusion.4
  188.8 47.9 %psum.53 = f32[60,4]{0,1:T(4,128)S(1)} all-reduce(f32[60,4]{0,1:T(4,128)S(1)} %convolution_bitcast_fusion.4), channel_id=1, replica_groups=mesh['gx'=8,'gy'=4] {'gx','gy'}, use_global_device_ids=true, to_apply=%region_35.36 | all-reduce | flops 240 | bytes 1920 | tf_op jit(solution)/shard_map/psum | solution.py:192
  239.2 3.0 collective-permute-start.28
  244.3 4.5 %collective-permute-start.30 = (f32[4,6,1,64]{3,0,2,1:T(4,128)S(1)}, f32[4,6,1,64]{3,0,2,1:T(4,128)S(1)}, u32[]{:S(2)}, u32[]{:S(2)}) collective-permute-start(f32[4,6,1,64]{3,0,2,1:T(4,128)S(1)} %get-tuple-element.62), channel_id=1, source_target_pairs={{0,1},{1,2},{2,3},{4,5},{5,6},{6,7},{8,9},{9,10},{10,11},{12,13},{... | collective-permute-start | bytes 18440 | tf_op jit(solution)/shard_map/ppermute | solution.py:22
  250.9 44.2 %all-reduce.12 = (f32[12,12]{0,1:T(8,128)S(1)}, f32[12,12]{0,1:T(8,128)S(1)}) all-reduce(f32[12,12]{0,1:T(8,128)S(1)} %convolution_bitcast_fusion.1, f32[12,12]{0,1:T(8,128)S(1)} %convolution_bitcast_fusion.2), channel_id=1, replica_groups=mesh['gx'=8,'gy'=4] {'gx','gy'}, use_global_device_ids=true, to_apply=%region_39.40 | all-reduce | flops 288 | bytes 2304 | tf_op jit(solution)/shard_map/psum | solution.py:199
  (247 shorter events, 58.4 us)
Async XLA Ops:
  1.6 13.3 %collective-permute-start = (f32[1,8,64]{2,1,0:T(8,128)S(1)}, f32[1,8,64]{2,1,0:T(8,128)S(1)}, u32[]{:S(2)}, u32[]{:S(2)}) collective-permute-start(f32[1,8,64]{2,1,0:T(8,128)S(1)} %slice.492), channel_id=1, source_target_pairs={{0,4},{4,8},{8,12},{12,16},{16,20},{20,24},{24,28},{1,5},{5,9},{9,... | collective-permute-start | bytes 6152 | tf_op jit(solution)/shard_map/ppermute | solution.py:22
  4.1 10.9 %collective-permute-start.1 = (f32[1,8,64]{2,1,0:T(8,128)S(1)}, f32[1,8,64]{2,1,0:T(8,128)S(1)}, u32[]{:S(2)}, u32[]{:S(2)}) collective-permute-start(f32[1,8,64]{2,1,0:T(8,128)S(1)} %slice.495), channel_id=1, source_target_pairs={{4,0},{8,4},{12,8},{16,12},{20,16},{24,20},{28,24},{5,1},{9,5},{13... | collective-permute-start | bytes 6152 | tf_op jit(solution)/shard_map/ppermute | solution.py:25
  6.4 34.1 %collective-permute-start.5 = (f32[8,1,8,64]{3,0,2,1:T(8,128)S(1)}, f32[8,1,8,64]{3,0,2,1:T(8,128)S(1)}, u32[]{:S(2)}, u32[]{:S(2)}) collective-permute-start(f32[8,1,8,64]{3,0,2,1:T(8,128)S(1)} %get-tuple-element.61), channel_id=1, source_target_pairs={{4,0},{8,4},{12,8},{16,12},{20,16},{24,20},{28,24},{5,1},{9,5},{13... | collective-permute-start | bytes 49160 | tf_op jit(solution)/shard_map/ppermute | solution.py:25
  7.7 32.8 %collective-permute-start.4 = (f32[8,1,8,64]{3,0,2,1:T(8,128)S(1)}, f32[8,1,8,64]{3,0,2,1:T(8,128)S(1)}, u32[]{:S(2)}, u32[]{:S(2)}) collective-permute-start(f32[8,1,8,64]{3,0,2,1:T(8,128)S(1)} %get-tuple-element.60), channel_id=1, source_target_pairs={{0,4},{4,8},{8,12},{12,16},{16,20},{20,24},{24,28},{1,5},{5,9},{9,... | collective-permute-start | bytes 49160 | tf_op jit(solution)/shard_map/ppermute | solution.py:22
  15.0 5.2 %collective-permute-start.2 = (f32[6,1,64]{2,1,0:T(1,128)S(1)}, f32[6,1,64]{2,1,0:T(1,128)S(1)}, u32[]{:S(2)}, u32[]{:S(2)}) collective-permute-start(f32[6,1,64]{2,1,0:T(1,128)S(1)} %get-tuple-element.82), channel_id=1, source_target_pairs={{0,1},{1,2},{2,3},{4,5},{5,6},{6,7},{8,9},{9,10},{10,11},{12,13},{... | collective-permute-start | bytes 4616 | tf_op jit(solution)/shard_map/ppermute | solution.py:22
  18.5 5.5 %collective-permute-start.3 = (f32[6,1,64]{2,1,0:T(1,128)S(1)}, f32[6,1,64]{2,1,0:T(1,128)S(1)}, u32[]{:S(2)}, u32[]{:S(2)}) collective-permute-start(f32[6,1,64]{2,1,0:T(1,128)S(1)} %get-tuple-element.81), channel_id=1, source_target_pairs={{1,0},{2,1},{3,2},{5,4},{6,5},{7,6},{9,8},{10,9},{11,10},{13,12},{... | collective-permute-start | bytes 4616 | tf_op jit(solution)/shard_map/ppermute | solution.py:25
  40.6 5.9 %collective-permute-start.7 = (f32[8,6,1,64]{3,0,2,1:T(8,128)S(1)}, f32[8,6,1,64]{3,0,2,1:T(8,128)S(1)}, u32[]{:S(2)}, u32[]{:S(2)}) collective-permute-start(f32[8,6,1,64]{3,0,2,1:T(8,128)S(1)} %get-tuple-element.53), channel_id=1, source_target_pairs={{1,0},{2,1},{3,2},{5,4},{6,5},{7,6},{9,8},{10,9},{11,10},{13,12},{... | collective-permute-start | bytes 36872 | tf_op jit(solution)/shard_map/ppermute | solution.py:25
  41.9 6.1 %collective-permute-start.6 = (f32[8,6,1,64]{3,0,2,1:T(8,128)S(1)}, f32[8,6,1,64]{3,0,2,1:T(8,128)S(1)}, u32[]{:S(2)}, u32[]{:S(2)}) collective-permute-start(f32[8,6,1,64]{3,0,2,1:T(8,128)S(1)} %get-tuple-element.52), channel_id=1, source_target_pairs={{0,1},{1,2},{2,3},{4,5},{5,6},{6,7},{8,9},{9,10},{10,11},{12,13},{... | collective-permute-start | bytes 36872 | tf_op jit(solution)/shard_map/ppermute | solution.py:22
  92.5 4.4 %collective-permute-start.9 = (f32[4,1,8,64]{3,0,2,1:T(4,128)S(1)}, f32[4,1,8,64]{3,0,2,1:T(4,128)S(1)}, u32[]{:S(2)}, u32[]{:S(2)}) collective-permute-start(f32[4,1,8,64]{3,0,2,1:T(4,128)S(1)} %get-tuple-element.73), channel_id=1, source_target_pairs={{4,0},{8,4},{12,8},{16,12},{20,16},{24,20},{28,24},{5,1},{9,5},{13... | collective-permute-start | bytes 24584 | tf_op jit(solution)/shard_map/ppermute | solution.py:25
  93.8 3.9 %collective-permute-start.8 = (f32[4,1,8,64]{3,0,2,1:T(4,128)S(1)}, f32[4,1,8,64]{3,0,2,1:T(4,128)S(1)}, u32[]{:S(2)}, u32[]{:S(2)}) collective-permute-start(f32[4,1,8,64]{3,0,2,1:T(4,128)S(1)} %get-tuple-element.72), channel_id=1, source_target_pairs={{0,4},{4,8},{8,12},{12,16},{16,20},{20,24},{24,28},{1,5},{5,9},{9,... | collective-permute-start | bytes 24584 | tf_op jit(solution)/shard_map/ppermute | solution.py:22
  97.6 5.9 %collective-permute-start.11 = (f32[4,6,1,64]{3,0,2,1:T(4,128)S(1)}, f32[4,6,1,64]{3,0,2,1:T(4,128)S(1)}, u32[]{:S(2)}, u32[]{:S(2)}) collective-permute-start(f32[4,6,1,64]{3,0,2,1:T(4,128)S(1)} %get-tuple-element.67), channel_id=1, source_target_pairs={{1,0},{2,1},{3,2},{5,4},{6,5},{7,6},{9,8},{10,9},{11,10},{13,12},{... | collective-permute-start | bytes 18440 | tf_op jit(solution)/shard_map/ppermute | solution.py:25
  98.9 5.9 %collective-permute-start.10 = (f32[4,6,1,64]{3,0,2,1:T(4,128)S(1)}, f32[4,6,1,64]{3,0,2,1:T(4,128)S(1)}, u32[]{:S(2)}, u32[]{:S(2)}) collective-permute-start(f32[4,6,1,64]{3,0,2,1:T(4,128)S(1)} %get-tuple-element.66), channel_id=1, source_target_pairs={{0,1},{1,2},{2,3},{4,5},{5,6},{6,7},{8,9},{9,10},{10,11},{12,13},{... | collective-permute-start | bytes 18440 | tf_op jit(solution)/shard_map/ppermute | solution.py:22
  105.6 4.7 %collective-permute-start.13 = (f32[4,1,4,32]{2,3,1,0:T(8,128)S(1)}, f32[4,1,4,32]{2,3,1,0:T(8,128)S(1)}, u32[]{:S(2)}, u32[]{:S(2)}) collective-permute-start(f32[4,1,4,32]{2,3,1,0:T(8,128)S(1)} %get-tuple-element.59), channel_id=1, source_target_pairs={{4,0},{8,4},{12,8},{16,12},{20,16},{24,20},{28,24},{5,1},{9,5},{13... | collective-permute-start | bytes 6152 | tf_op jit(solution)/shard_map/ppermute | solution.py:25
  106.9 4.2 %collective-permute-start.12 = (f32[4,1,4,32]{2,3,1,0:T(8,128)S(1)}, f32[4,1,4,32]{2,3,1,0:T(8,128)S(1)}, u32[]{:S(2)}, u32[]{:S(2)}) collective-permute-start(f32[4,1,4,32]{2,3,1,0:T(8,128)S(1)} %get-tuple-element.58), channel_id=1, source_target_pairs={{0,4},{4,8},{8,12},{12,16},{16,20},{20,24},{24,28},{1,5},{5,9},{9,... | collective-permute-start | bytes 6152 | tf_op jit(solution)/shard_map/ppermute | solution.py:22
  111.3 8.3 %collective-permute-start.15 = (f32[4,4,1,32]{2,3,1,0:T(8,128)S(1)}, f32[4,4,1,32]{2,3,1,0:T(8,128)S(1)}, u32[]{:S(2)}, u32[]{:S(2)}) collective-permute-start(f32[4,4,1,32]{2,3,1,0:T(8,128)S(1)} %get-tuple-element.51), channel_id=1, source_target_pairs={{1,0},{2,1},{3,2},{5,4},{6,5},{7,6},{9,8},{10,9},{11,10},{13,12},{... | collective-permute-start | bytes 6152 | tf_op jit(solution)/shard_map/ppermute | solution.py:25
  112.6 8.4 %collective-permute-start.14 = (f32[4,4,1,32]{2,3,1,0:T(8,128)S(1)}, f32[4,4,1,32]{2,3,1,0:T(8,128)S(1)}, u32[]{:S(2)}, u32[]{:S(2)}) collective-permute-start(f32[4,4,1,32]{2,3,1,0:T(8,128)S(1)} %get-tuple-element.50), channel_id=1, source_target_pairs={{0,1},{1,2},{2,3},{4,5},{5,6},{6,7},{8,9},{9,10},{10,11},{12,13},{... | collective-permute-start | bytes 6152 | tf_op jit(solution)/shard_map/ppermute | solution.py:22
  136.4 4.3 %collective-permute-start.17 = (f32[4,1,8,16]{3,0,2,1:T(4,128)S(1)}, f32[4,1,8,16]{3,0,2,1:T(4,128)S(1)}, u32[]{:S(2)}, u32[]{:S(2)}) collective-permute-start(f32[4,1,8,16]{3,0,2,1:T(4,128)S(1)} %maximum_bitcast_fusion), channel_id=1, source_target_pairs={{4,0},{8,4},{12,8},{16,12},{20,16},{24,20},{28,24},{5,1},{9,5},{13... | collective-permute-start | bytes 6152 | tf_op jit(solution)/shard_map/ppermute | solution.py:25
  137.7 3.9 %collective-permute-start.16 = (f32[4,1,8,16]{3,0,2,1:T(4,128)S(1)}, f32[4,1,8,16]{3,0,2,1:T(4,128)S(1)}, u32[]{:S(2)}, u32[]{:S(2)}) collective-permute-start(f32[4,1,8,16]{3,0,2,1:T(4,128)S(1)} %maximum_bitcast_fusion), channel_id=1, source_target_pairs={{0,4},{4,8},{8,12},{12,16},{16,20},{20,24},{24,28},{1,5},{5,9},{9,... | collective-permute-start | bytes 6152 | tf_op jit(solution)/shard_map/ppermute | solution.py:22
  141.7 11.7 %collective-permute-start.19 = (f32[4,1,8,16]{3,0,2,1:T(4,128)S(1)}, f32[4,1,8,16]{3,0,2,1:T(4,128)S(1)}, u32[]{:S(2)}, u32[]{:S(2)}) collective-permute-start(f32[4,1,8,16]{3,0,2,1:T(4,128)S(1)} %divide_add_fusion.1), channel_id=1, source_target_pairs={{4,0},{8,4},{12,8},{16,12},{20,16},{24,20},{28,24},{5,1},{9,5},{13... | collective-permute-start | bytes 6152 | tf_op jit(solution)/shard_map/ppermute | solution.py:25
  143.0 11.2 %collective-permute-start.18 = (f32[4,1,8,16]{3,0,2,1:T(4,128)S(1)}, f32[4,1,8,16]{3,0,2,1:T(4,128)S(1)}, u32[]{:S(2)}, u32[]{:S(2)}) collective-permute-start(f32[4,1,8,16]{3,0,2,1:T(4,128)S(1)} %divide_add_fusion.1), channel_id=1, source_target_pairs={{0,4},{4,8},{8,12},{12,16},{16,20},{20,24},{24,28},{1,5},{5,9},{9,... | collective-permute-start | bytes 6152 | tf_op jit(solution)/shard_map/ppermute | solution.py:22
  154.5 6.2 %collective-permute-start.21 = (f32[4,1,4,32]{2,3,1,0:T(8,128)S(1)}, f32[4,1,4,32]{2,3,1,0:T(8,128)S(1)}, u32[]{:S(2)}, u32[]{:S(2)}) collective-permute-start(f32[4,1,4,32]{2,3,1,0:T(8,128)S(1)} %get-tuple-element.57), channel_id=1, source_target_pairs={{4,0},{8,4},{12,8},{16,12},{20,16},{24,20},{28,24},{5,1},{9,5},{13... | collective-permute-start | bytes 6152 | tf_op jit(solution)/shard_map/ppermute | solution.py:25
  155.8 5.8 %collective-permute-start.20 = (f32[4,1,4,32]{2,3,1,0:T(8,128)S(1)}, f32[4,1,4,32]{2,3,1,0:T(8,128)S(1)}, u32[]{:S(2)}, u32[]{:S(2)}) collective-permute-start(f32[4,1,4,32]{2,3,1,0:T(8,128)S(1)} %get-tuple-element.56), channel_id=1, source_target_pairs={{0,4},{4,8},{8,12},{12,16},{16,20},{20,24},{24,28},{1,5},{5,9},{9,... | collective-permute-start | bytes 6152 | tf_op jit(solution)/shard_map/ppermute | solution.py:22
  161.7 9.3 %collective-permute-start.23 = (f32[4,4,1,32]{2,3,1,0:T(8,128)S(1)}, f32[4,4,1,32]{2,3,1,0:T(8,128)S(1)}, u32[]{:S(2)}, u32[]{:S(2)}) collective-permute-start(f32[4,4,1,32]{2,3,1,0:T(8,128)S(1)} %get-tuple-element.49), channel_id=1, source_target_pairs={{1,0},{2,1},{3,2},{5,4},{6,5},{7,6},{9,8},{10,9},{11,10},{13,12},{... | collective-permute-start | bytes 6152 | tf_op jit(solution)/shard_map/ppermute | solution.py:25
  163.0 9.7 %collective-permute-start.22 = (f32[4,4,1,32]{2,3,1,0:T(8,128)S(1)}, f32[4,4,1,32]{2,3,1,0:T(8,128)S(1)}, u32[]{:S(2)}, u32[]{:S(2)}) collective-permute-start(f32[4,4,1,32]{2,3,1,0:T(8,128)S(1)} %get-tuple-element.48), channel_id=1, source_target_pairs={{0,1},{1,2},{2,3},{4,5},{5,6},{6,7},{8,9},{9,10},{10,11},{12,13},{... | collective-permute-start | bytes 6152 | tf_op jit(solution)/shard_map/ppermute | solution.py:22
  173.6 5.5 %collective-permute-start.25 = (f32[4,1,8,64]{3,0,2,1:T(4,128)S(1)}, f32[4,1,8,64]{3,0,2,1:T(4,128)S(1)}, u32[]{:S(2)}, u32[]{:S(2)}) collective-permute-start(f32[4,1,8,64]{3,0,2,1:T(4,128)S(1)} %get-tuple-element.71), channel_id=1, source_target_pairs={{4,0},{8,4},{12,8},{16,12},{20,16},{24,20},{28,24},{5,1},{9,5},{13... | collective-permute-start | bytes 24584 | tf_op jit(solution)/shard_map/ppermute | solution.py:25
  174.9 5.0 %collective-permute-start.24 = (f32[4,1,8,64]{3,0,2,1:T(4,128)S(1)}, f32[4,1,8,64]{3,0,2,1:T(4,128)S(1)}, u32[]{:S(2)}, u32[]{:S(2)}) collective-permute-start(f32[4,1,8,64]{3,0,2,1:T(4,128)S(1)} %get-tuple-element.70), channel_id=1, source_target_pairs={{0,4},{4,8},{8,12},{12,16},{16,20},{20,24},{24,28},{1,5},{5,9},{9,... | collective-permute-start | bytes 24584 | tf_op jit(solution)/shard_map/ppermute | solution.py:22
  179.9 6.2 %collective-permute-start.27 = (f32[4,6,1,64]{3,0,2,1:T(4,128)S(1)}, f32[4,6,1,64]{3,0,2,1:T(4,128)S(1)}, u32[]{:S(2)}, u32[]{:S(2)}) collective-permute-start(f32[4,6,1,64]{3,0,2,1:T(4,128)S(1)} %get-tuple-element.65), channel_id=1, source_target_pairs={{1,0},{2,1},{3,2},{5,4},{6,5},{7,6},{9,8},{10,9},{11,10},{13,12},{... | collective-permute-start | bytes 18440 | tf_op jit(solution)/shard_map/ppermute | solution.py:25
  181.2 6.1 %collective-permute-start.26 = (f32[4,6,1,64]{3,0,2,1:T(4,128)S(1)}, f32[4,6,1,64]{3,0,2,1:T(4,128)S(1)}, u32[]{:S(2)}, u32[]{:S(2)}) collective-permute-start(f32[4,6,1,64]{3,0,2,1:T(4,128)S(1)} %get-tuple-element.64), channel_id=1, source_target_pairs={{0,1},{1,2},{2,3},{4,5},{5,6},{6,7},{8,9},{9,10},{10,11},{12,13},{... | collective-permute-start | bytes 18440 | tf_op jit(solution)/shard_map/ppermute | solution.py:22
  237.9 4.3 %collective-permute-start.29 = (f32[4,1,8,64]{3,0,2,1:T(4,128)S(1)}, f32[4,1,8,64]{3,0,2,1:T(4,128)S(1)}, u32[]{:S(2)}, u32[]{:S(2)}) collective-permute-start(f32[4,1,8,64]{3,0,2,1:T(4,128)S(1)} %get-tuple-element.69), channel_id=1, source_target_pairs={{4,0},{8,4},{12,8},{16,12},{20,16},{24,20},{28,24},{5,1},{9,5},{13... | collective-permute-start | bytes 24584 | tf_op jit(solution)/shard_map/ppermute | solution.py:25
  239.2 3.9 %collective-permute-start.28 = (f32[4,1,8,64]{3,0,2,1:T(4,128)S(1)}, f32[4,1,8,64]{3,0,2,1:T(4,128)S(1)}, u32[]{:S(2)}, u32[]{:S(2)}) collective-permute-start(f32[4,1,8,64]{3,0,2,1:T(4,128)S(1)} %get-tuple-element.68), channel_id=1, source_target_pairs={{0,4},{4,8},{8,12},{12,16},{16,20},{20,24},{24,28},{1,5},{5,9},{9,... | collective-permute-start | bytes 24584 | tf_op jit(solution)/shard_map/ppermute | solution.py:22
  243.0 6.3 %collective-permute-start.31 = (f32[4,6,1,64]{3,0,2,1:T(4,128)S(1)}, f32[4,6,1,64]{3,0,2,1:T(4,128)S(1)}, u32[]{:S(2)}, u32[]{:S(2)}) collective-permute-start(f32[4,6,1,64]{3,0,2,1:T(4,128)S(1)} %get-tuple-element.63), channel_id=1, source_target_pairs={{1,0},{2,1},{3,2},{5,4},{6,5},{7,6},{9,8},{10,9},{11,10},{13,12},{... | collective-permute-start | bytes 18440 | tf_op jit(solution)/shard_map/ppermute | solution.py:25
  244.3 5.9 %collective-permute-start.30 = (f32[4,6,1,64]{3,0,2,1:T(4,128)S(1)}, f32[4,6,1,64]{3,0,2,1:T(4,128)S(1)}, u32[]{:S(2)}, u32[]{:S(2)}) collective-permute-start(f32[4,6,1,64]{3,0,2,1:T(4,128)S(1)} %get-tuple-element.62), channel_id=1, source_target_pairs={{0,1},{1,2},{2,3},{4,5},{5,6},{6,7},{8,9},{9,10},{10,11},{12,13},{... | collective-permute-start | bytes 18440 | tf_op jit(solution)/shard_map/ppermute | solution.py:22
  (4 other events, 25.9 us)
where the time goes:
time: 316 us; the launch traced here: 315 us
  blocking collectives  162 us (51%)
  starting transfers between devices  91.7 us (29%)
  waiting for transfers between devices  23.5 us (7%)
  other arithmetic  14 us (4%)
  matrix products  13.8 us (4%)
  local copies, waits for them, and re-layouts  7.32 us (2%)
    ppermute x16, starting transfers between devices, extended(): lax.ppermute(lax.slice_in_dim(block, block.shape[dim] - width, None, axis...  71.1 us
    psum x1, blocking collectives, on_device(): lax.psum(correlation_part, ('gx', 'gy')) / cell_count  47.9 us
    psum x1, blocking collectives, on_device(): mass_sum, stiff_sum = lax.psum((mass_part, stiff_part), ('gx', 'gy'))  44.2 us
    psum x1, blocking collectives, on_device(): lax.psum((top_part, norm_part, image_part, mode_part), ('gx', 'gy'))  41.7 us
    ppermute x16, starting transfers between devices, extended(): lax.ppermute(lax.slice_in_dim(block, 0, width, axis=dim), axis, backward)  20.7 us
    all_gather x1, blocking collectives, coarse_solve(): gathered = lax.all_gather(source, 'gy', axis=2, tiled=True)  14.7 us
    ppermute x16, waiting for transfers between devices, extended(): lax.ppermute(lax.slice_in_dim(block, block.shape[dim] - width, None, axis...  13.9 us
    all_gather x1, blocking collectives, on_device(): coarse_coeffs = lax.all_gather(coarse_coeffs, 'gy', axis=2, tiled=True)  13.4 us
  transfers between devices with their start and end apart: 32, of which 16 were waited for; matrix products, arithmetic and copies ran while one was open for 2% of the time, Pallas kernels for 0%

commit v1 on v0

v1 whole, which is shorter than its diff:
```python
import functools

import jax
import jax.numpy as jnp
from jax import lax
from jax.experimental import pallas as pl
from jax.experimental.pallas import tpu as pltpu
from jax.sharding import PartitionSpec as P

NZ = 64
ACTIVE = 4
SWEEPS = 3
RITZ = 3
OMEGA = 0.6
EPSILON = 1e-06
PRECISE = lax.Precision.HIGHEST
F32 = jnp.float32
REACH = SWEEPS


def iota(shape, dim):
    return lax.broadcasted_iota(jnp.int32, shape, dim)


def nt(a, b):
    return lax.dot_general(a, b, (((1,), (1,)), ((), ())), precision=PRECISE, preferred_element_type=F32)


def nn(a, b):
    return lax.dot_general(a, b, (((1,), (0,)), ((), ())), precision=PRECISE, preferred_element_type=F32)


def lanes(u, by):
    return pltpu.roll(u, by % 128, u.ndim - 1)


def subs(u, by):
    return pltpu.roll(u, by % 8, u.ndim - 2)


def face_value(a, b):
    both = (a > 0) & (b > 0)
    return jnp.where(both, 2.0 * a * b / jnp.where(both, a + b, 1.0), 2.0 * (a + b))


class Marks:
    def __init__(self):
        lane = iota((8, 128), 1)
        sub = iota((8, 128), 0)
        self.lane = lane
        self.sub = sub
        self.z = lane % NZ
        self.half0 = lane < 64
        self.par0 = sub < 4
        self.even = lane % 2 == 0
        self.quad = lane % 4 < 2


def neighbours(m, u):
    inner = u[1:-1, 1:-1]
    zl = jnp.where(m.z == 0, 0.0, lanes(inner, 1))
    zu = jnp.where(m.z == NZ - 1, 0.0, lanes(inner, -1))
    flip = lanes(u[1:-1], 64)
    yl = jnp.where(m.half0, flip[:, :-2], flip[:, 1:-1])
    yu = jnp.where(m.half0, flip[:, 1:-1], flip[:, 2:])
    turn = subs(u[:, 1:-1], 4)
    xl = jnp.where(m.par0, turn[:-2], turn[1:-1])
    xu = jnp.where(m.par0, turn[1:-1], turn[2:])
    return xl, xu, yl, yu, zl, zu


def total(parts):
    out = parts[0]
    for part in parts[1:]:
        out = out + part
    return out


def fine_coef(m, k):
    inner = k[1:-1, 1:-1]
    faces = [face_value(near, inner) for near in neighbours(m, k)]
    return [total(faces)] + faces


def stencil(m, u, coef):
    near = neighbours(m, u)
    return coef[0] * u[1:-1, 1:-1] - total([c * v for c, v in zip(coef[1:], near)])


def inverse(diag, inside):
    return jnp.where(inside, OMEGA / jnp.where(inside, diag, 1.0), 0.0)


def pair_x(u):
    return u + subs(u, 4)


def pair_y(u):
    return u + lanes(u, 64)


def pair_z(m, u):
    return u + jnp.where(m.even, lanes(u, -1), lanes(u, 1))


def pair_z2(m, u):
    return u + jnp.where(m.quad, lanes(u, -2), lanes(u, 2))


def middle_coef(m, c):
    xl = pair_z(m, pair_y(jnp.where(m.par0, c[1], subs(c[1], 4))))
    xu = pair_z(m, pair_y(jnp.where(m.par0, subs(c[2], 4), c[2])))
    yl = pair_z(m, pair_x(jnp.where(m.half0, c[3], lanes(c[3], 64))))
    yu = pair_z(m, pair_x(jnp.where(m.half0, lanes(c[4], 64), c[4])))
    zl = pair_y(pair_x(jnp.where(m.even, c[5], lanes(c[5], 1))))
    zu = pair_y(pair_x(jnp.where(m.even, lanes(c[6], -1), c[6])))
    faces = [xl, xu, yl, yu, zl, zu]
    return [total(faces)] + faces


def middle_stencil(m, u, coef):
    inner = u[1:-1, 1:-1]
    zl = jnp.where(m.z < 2, 0.0, lanes(inner, 2))
    zu = jnp.where(m.z >= NZ - 2, 0.0, lanes(inner, -2))
    near = [u[:-2, 1:-1], u[2:, 1:-1], u[1:-1, :-2], u[1:-1, 2:], zl, zu]
    return coef[0] * inner - total([c * v for c, v in zip(coef[1:], near)])


def coarse_pack(m, mid):
    _, xl, xu, yl, yu, zl, zu = mid
    out = jnp.zeros((8, 128), F32)
    for q in range(2):
        a, b = 2 * q, 2 * q + 1
        faces = [
            pair_z2(m, xl[0, a] + xl[0, b]),
            pair_z2(m, xu[1, a] + xu[1, b]),
            pair_z2(m, yl[0, a] + yl[1, a]),
            pair_z2(m, yu[0, b] + yu[1, b]),
        ]
        low = zl[0, a] + zl[0, b] + zl[1, a] + zl[1, b]
        high = zu[0, a] + zu[0, b] + zu[1, a] + zu[1, b]
        faces.append(jnp.where(m.quad, low, lanes(low, 2)))
        faces.append(jnp.where(m.quad, lanes(high, -2), high))
        for k in range(6):
            spot = (m.sub == 4 * q + k % 4) & (m.half0 if k < 4 else ~m.half0)
            out = jnp.where(spot, faces[k], out)
    return out


def flat(u):
    return jnp.concatenate([u[x, y] for x in range(2) for y in range(4)], axis=1)


def unflat(u):
    tiles = [u[:, 128 * i : 128 * (i + 1)] for i in range(8)]
    return jnp.stack([jnp.stack(tiles[:4]), jnp.stack(tiles[4:])])


def fold_locked(m, g):
    g = jnp.where(m.par0 == m.half0, g, 0.0)
    return pair_y(pair_x(g))


def spread_locked(m, c):
    return jnp.where(m.par0 == m.half0, c, 0.0)


def kernel(
    ngx,
    ngy,
    modes_ref,
    dirs_ref,
    locked_ref,
    class_ref,
    table_ref,
    count_ref,
    new_modes_ref,
    new_dirs_ref,
    ritz_ref,
    corr_ref,
    kh,
    xp,
    e0h,
    e1h,
    wh,
    ccg,
    r2g,
    e2s,
    lst,
    by1,
    bx1,
    by2,
    bx2,
    by3,
    bx3,
    hs,
    hr,
    rs,
    rr,
    cs,
    cr,
):
    m = Marks()
    gx, gy = lax.axis_index("gx"), lax.axis_index("gy")
    count = ngx * ngy
    cells = float(4 * 512 * count)
    pending = []

    for buf in (kh, xp, e0h, e1h, wh, ccg, r2g, e2s):
        buf[...] = jnp.zeros(buf.shape, F32)

    barrier = pltpu.get_barrier_semaphore()
    me = gx * ngy + gy

    def greet(i, carry):
        other = lax.rem(me + i, count)
        pl.semaphore_signal(
            barrier, inc=1, device_id=(other // ngy, lax.rem(other, ngy)), device_id_type=pl.DeviceIdType.MESH
        )
        return carry

    lax.fori_loop(1, count, greet, 0)

    def remote(src, dst, send, recv, tx, ty):
        return pltpu.make_async_remote_copy(
            src_ref=src, dst_ref=dst, send_sem=send, recv_sem=recv, device_id=(tx, ty),
            device_id_type=pl.DeviceIdType.MESH,
        )

    def inside(tx, ty):
        return (tx >= 0) & (tx < ngx) & (ty >= 0) & (ty < ngy)

    def halo(slot, view, w, corners):
        def span(d, n):
            if d > 0:
                return pl.ds(n, w), pl.ds(0, w)
            if d < 0:
                return pl.ds(w, w), pl.ds(w + n, w)
            return pl.ds(w, n), pl.ds(w, n)

        copies = []
        for dx in (-1, 0, 1):
            for dy in (-1, 0, 1):
                if (dx, dy) == (0, 0) or (dx and dy and not corners):
                    continue
                (sx, tx), (sy, ty) = span(dx, 2), span(dy, 4)
                n = (dx + 1) * 3 + dy + 1
                copy = remote(view(sx, sy), view(tx, ty), hs.at[slot, n], hr.at[slot, n], gx + dx, gy + dy)
                to, frm = inside(gx + dx, gy + dy), inside(gx - dx, gy - dy)
                pl.when(to)(copy.start)
                copies.append((copy, frm))
                pending.append((copy, to))

        def arrive():
            for copy, frm in copies:
                pl.when(frm)(copy.wait_recv)

        return arrive

    def share(slot, buf, mine, n, axis, view):
        copies = []
        for i in range(1, n):
            to, frm = lax.rem(mine + i, n), lax.rem(mine + n - i, n)
            where = (gx, to) if axis == "gy" else (to, gy)
            back = (gx, frm) if axis == "gy" else (frm, gy)
            copy = remote(view(buf, mine), view(buf, mine), rs.at[slot, i], rr.at[slot, i], *where)
            copy.start()
            pending.append((copy, None))
            copies.append(remote(view(buf, frm), view(buf, frm), rs.at[slot, i], rr.at[slot, i], *back))

        def arrive():
            for copy in copies:
                copy.wait_recv()

        return arrive

    def reduce_start(slot, val, bufy):
        bufy[gy] = val
        return share(slot, bufy, gy, ngy, "gy", lambda b, i: b.at[i])

    def reduce_end(slot, first, bufy, bufx):
        first()
        bufx[gx] = total([bufy[j] for j in range(ngy)])
        share(slot + 1, bufx, gx, ngx, "gx", lambda b, i: b.at[i])()
        return total([bufx[j] for j in range(ngx)])

    def gather_start(slot, buf, val):
        buf[REACH, gy] = val
        return share(slot, buf, gy, ngy, "gy", lambda b, i: b.at[REACH, i])

    def gather_next(slot, first, buf):
        first()
        copies = []
        for d in range(-REACH, REACH + 1):
            if d == 0:
                continue
            copy = remote(
                buf.at[REACH], buf.at[REACH - d], cs.at[slot, d + REACH], cr.at[slot, d + REACH], gx + d, gy
            )
            to, frm = inside(gx + d, gy), inside(gx - d, gy)
            pl.when(to)(copy.start)
            copies.append((copy, frm))
            pending.append((copy, to))

        def arrive():
            for copy, frm in copies:
                pl.when(frm)(copy.wait_recv)

        return arrive

    classes = class_ref[...]
    conduct = jnp.zeros(classes.shape, F32)
    for c in range(table_ref.shape[0]):
        conduct = jnp.where(classes == c, table_ref[c], conduct)
    for x in range(4):
        for y in range(4):
            cut = slice(128 * y, 128 * (y + 1))
            rows = pl.ds(4 * (x % 2), 4)
            kh[2 + x // 2, 2 + y, rows, :] = jnp.broadcast_to(conduct[x : x + 1, cut], (4, 128))
            xp[0, 1 + x // 2, 1 + y, rows, :] = modes_ref[:, x, cut]
            xp[1, 1 + x // 2, 1 + y, rows, :] = dirs_ref[:, x, cut]
    pl.semaphore_wait(barrier, count - 1)
    arrive_k = halo(0, lambda a, b: kh.at[a, b], 2, True)
    arrive_xp = halo(1, lambda a, b: xp.at[:, a, b], 1, False)

    nl = locked_ref.shape[0]
    for x in range(4):
        for y in range(4):
            cut = slice(128 * y, 128 * (y + 1))
            to = pl.ds(128 * ((x // 2) * 4 + y), 128)
            lst[pl.ds(64 * (x % 2), nl), to] = locked_ref[:, x, cut]
            lst[pl.ds(64 * (x % 2) + nl, 4), to] = modes_ref[:, x, cut]

    own_x = xp[0, 1:3, 1:5]
    own_p = xp[1, 1:3, 1:5]
    x8 = flat(own_x)
    mode_dots = fold_locked(m, nt(x8, lst[...]))

    arrive_k()
    arrive_xp()
    own_coef = fine_coef(m, kh[1:5, 1:7])
    image_x = stencil(m, xp[0], own_coef)
    image_x8 = flat(image_x)
    image_dots = fold_locked(m, nt(image_x8, lst[...]))
    first = reduce_start(0, jnp.where(m.half0, image_dots, mode_dots), by1)

    wide = fine_coef(m, kh[...])
    in_grid = kh[1:5, 1:7] > 0
    dinv0 = inverse(wide[0], in_grid)
    mid = middle_coef(m, wide)
    dinv1 = inverse(mid[0], in_grid)
    own_mid = [c[1:3, 1:5] for c in mid]
    first_c = gather_start(6, ccg, coarse_pack(m, own_mid))
    image_p = stencil(m, xp[1], own_coef)

    sums = reduce_end(0, first, by1, bx1)
    arrive_c = gather_next(0, first_c, ccg)

    f_of = m.sub % 4
    top = jnp.sum(jnp.where(m.lane == nl + f_of, sums, 0.0), axis=1, keepdims=True)
    norm = jnp.sum(jnp.where(m.lane == 64 + nl + f_of, sums, 0.0), axis=1, keepdims=True)
    rayleigh = top / cells / (norm / cells + EPSILON)
    swapped = lanes(sums, 64)
    image_sum = jnp.where(m.half0, sums, swapped)
    mode_sum = jnp.where(m.half0, swapped, sums)
    j_of = m.lane % 64
    in_use = (j_of < count_ref[0]) & (j_of < nl)
    coupling = jnp.where(in_use, (image_sum - mode_sum * rayleigh) / cells, 0.0)
    coupling = jnp.where(j_of == nl + f_of, rayleigh, coupling)
    residual = image_x - unflat(nn(spread_locked(m, coupling), lst[...]))

    e0h[1:3, 1:5] = residual * dinv0[1:3, 1:5]
    arrive_e0 = halo(2, lambda a, b: e0h.at[a, b], 1, False)
    arrive_c()
    lines = 2 * ngy
    shift = 4.0 / float(lines * lines)
    faces = []
    for y in range(lines):
        tile = ccg[:, y // 2]
        other = lanes(tile, 64)
        low, high = jnp.where(m.half0, tile, other), jnp.where(m.half0, other, tile)
        row = 4 * (y % 2)
        one = []
        for k in range(6):
            src = low if k < 4 else high
            one.append(jnp.broadcast_to(src[:, row + k % 4 : row + k % 4 + 1], (2 * REACH + 1, 4, 128)))
        faces.append(one)
    z4 = m.z[:4]
    pivots, uppers, diags, dinv2 = [], [], [], []
    for y in range(lines):
        xl, xu, yl, yu, zl, zu = faces[y]
        diag = xl + xu + yl + yu + zl + zu
        known = diag > 0
        main = yl + yu + shift * (xl + xu + zl + zu)
        if y:
            main = main - yl * uppers[y - 1]
        piv = 1.0 / jnp.where(known, main, 1.0)
        pivots.append(piv)
        uppers.append(yu * piv)
        diags.append(diag)
        dinv2.append(inverse(diag, known))
        faces[y][4] = jnp.where(z4 < 4, 0.0, zl)
        faces[y][5] = jnp.where(z4 >= NZ - 4, 0.0, zu)

    arrive_e0()
    r1 = residual - stencil(m, e0h[...], own_coef)
    r1 = pair_z(m, pair_y(pair_x(r1)))
    e1h[2:4, 2:6] = r1 * dinv1[1:3, 1:5]
    halo(3, lambda a, b: e1h.at[a, b], 2, True)()
    e1_wide = e1h[...]
    r2 = r1 - middle_stencil(m, e1_wide[1:5, 1:7], own_mid)
    r2 = r2[0] + r2[1]
    r2 = jnp.where(m.par0, r2[0] + r2[1], r2[2] + r2[3])
    first_r = gather_start(7, r2g, pair_z2(m, r2))
    gather_next(1, first_r, r2g)()

    source = [r2g[:, y // 2, 4 * (y % 2) : 4 * (y % 2) + 4] for y in range(lines)]
    held = []
    for y in range(lines):
        right = source[y] if y == 0 else source[y] + faces[y][2] * held[y - 1]
        held.append(right * pivots[y])
    for y in range(lines - 2, -1, -1):
        held[y] = held[y] + uppers[y] * held[y + 1]
    for sweep in range(1, SWEEPS):
        nxt = []
        for y in range(lines):
            cut = slice(sweep, 2 * REACH + 1 - sweep)
            c = [f[cut] for f in faces[y]]
            u = held[y]
            mid_u = u[1:-1]
            beside = c[0] * u[:-2] + c[1] * u[2:]
            if y:
                beside = beside + c[2] * held[y - 1][1:-1]
            if y < lines - 1:
                beside = beside + c[3] * held[y + 1][1:-1]
            beside = beside + c[4] * lanes(mid_u, 4) + c[5] * lanes(mid_u, -4)
            off = source[y][cut] - (diags[y][cut] * mid_u - beside)
            nxt.append(mid_u + dinv2[y][cut] * off)
        held = nxt
    for y in range(lines):
        e2s[1 + y] = held[y]
    near = e2s[pl.ds(2 * gy, 4)]
    near = jnp.concatenate([near, near], axis=2)

    e1_wide = jnp.stack(
        [jnp.stack([e1_wide[a, b] + near[b // 2, a // 2] for b in range(8)]) for a in range(6)]
    )
    e1 = e1_wide[1:5, 1:7] + e1h[1:5, 1:7] - dinv1 * middle_stencil(m, e1_wide, mid)
    e0 = e0h[...] + e1
    precond = e0[1:3, 1:5] + e0h[1:3, 1:5] - dinv0[1:3, 1:5] * stencil(m, e0, own_coef)

    precond8 = flat(precond)
    dots = fold_locked(m, nt(precond8, lst[...]))
    sums = reduce_end(2, reduce_start(2, dots, by2), by2, bx2)
    corr = jnp.where(in_use, sums / cells, 0.0)
    corr_ref[...] = corr.T[: corr_ref.shape[0], :ACTIVE]
    projected8 = precond8 - nn(spread_locked(m, corr), lst[...])
    wh[1:3, 1:5] = unflat(projected8)
    halo(4, lambda a, b: wh.at[a, b], 1, False)()
    image_w = stencil(m, wh[...], own_coef)

    trial = jnp.concatenate([x8, projected8, flat(own_p)], axis=0)
    images = jnp.concatenate([image_x8, flat(image_w), flat(image_p)], axis=0)
    mass = nt(trial, trial)
    stiff = 0.5 * (nt(trial, images) + nt(images, trial))
    both = jnp.concatenate([mass, jnp.zeros((24, 8), F32), stiff, jnp.zeros((24, 72), F32)], axis=1)
    row, col = iota((24, 128), 0), iota((24, 128), 1)
    both = jnp.where((row // 4) % 2 == (col // 4) % 2, both, 0.0)
    both = both + jnp.concatenate([subs(both[8 * i : 8 * i + 8], 4) for i in range(3)], axis=0)
    both = both + lanes(both, -4)
    sums = reduce_end(4, reduce_start(4, both, by3), by3, bx3) / cells

    real = row % 8 < 4
    table = jnp.where(real & (col < 64) & (col % 8 < 4), sums, 0.0)
    table = jnp.where(real & (col == row + 64), 1.0, table)
    pivots_at = [8 * g + f for g in range(3) for f in range(4)]

    def eliminate(work, order, rows):
        for k in order:
            pivot = work[k : k + 1, k : k + 1]
            scale = lax.rsqrt(pivot)
            line = work[k : k + 1, :] * scale
            factor = jnp.where(rows > k, work[:, k : k + 1] * scale, 0.0)
            work = jnp.where(rows == k, line, work - factor * line)
        return work

    work = eliminate(table, pivots_at, row)
    half = jnp.where(col < 24, lanes(work, -32), 0.0)
    linv = jnp.where(col < 24, lanes(work, -64), 0.0)
    reduced = 0.5 * (nt(half, linv) + nt(linv, half))
    reduced = jnp.concatenate([reduced, jnp.zeros((24, 104), F32)], axis=1)
    spectral = jnp.sum(jnp.where(row == col, reduced, 0.0), keepdims=True)
    raised = jnp.where((row == col) & real, spectral, 0.0) - reduced
    full = jnp.concatenate([raised, jnp.zeros((104, 128), F32)], axis=0)
    reduced_full = jnp.concatenate([reduced, jnp.zeros((104, 128), F32)], axis=0)
    basis = jnp.where(m.par0, raised[:8], 0.0)
    for step in range(RITZ - 1):
        basis = nn(basis, full)
    square = nt(basis, basis)
    small = jnp.concatenate([square, jnp.zeros((8, 120), F32)], axis=1) + lanes(basis, 32)
    small = eliminate(small, range(4), m.sub)
    basis = jnp.where((m.lane < 24) & m.par0, lanes(small, -32), 0.0)
    ritz = jnp.sum(basis * nn(basis, reduced_full), axis=1, keepdims=True)
    for k in range(ACTIVE):
        ritz_ref[k] = ritz[k, 0]
    linv_full = jnp.concatenate([linv, jnp.zeros((104, 128), F32)], axis=0)
    coef = nn(basis, linv_full)
    coef = coef + lanes(coef, 4)
    coef = coef + subs(coef, 4)
    coef = jnp.where(m.par0 == ((m.lane // 4) % 2 == 0), coef, 0.0)[:, :24]
    modes8 = nn(coef, trial)
    dirs8 = nn(coef[:, 8:], trial[8:])
    for x in range(4):
        for y in range(4):
            cut = slice(128 * y, 128 * (y + 1))
            frm = slice(128 * ((x // 2) * 4 + y), 128 * ((x // 2) * 4 + y + 1))
            rows = slice(4 * (x % 2), 4 * (x % 2) + 4)
            new_modes_ref[:, x, cut] = modes8[rows, frm]
            new_dirs_ref[:, x, cut] = dirs8[rows, frm]

    for copy, to in pending:
        if to is None:
            copy.wait_send()
        else:
            pl.when(to)(copy.wait_send)


def on_device(ngx, ngy, modes, directions, locked, perm_class, perm_table, locked_count):
    vmem = pl.BlockSpec(memory_space=pltpu.VMEM)
    smem = pl.BlockSpec(memory_space=pltpu.SMEM)
    dma = pltpu.SemaphoreType.DMA
    wide = 2 * REACH + 1
    return pl.pallas_call(
        functools.partial(kernel, ngx, ngy),
        out_shape=(
            jax.ShapeDtypeStruct(modes.shape, F32),
            jax.ShapeDtypeStruct(modes.shape, F32),
            jax.ShapeDtypeStruct((ACTIVE,), F32),
            jax.ShapeDtypeStruct((locked.shape[0], ACTIVE), F32),
        ),
        in_specs=[vmem, vmem, vmem, vmem, smem, smem],
        out_specs=(vmem, vmem, smem, vmem),
        scratch_shapes=[
            pltpu.VMEM((6, 8, 8, 128), F32),
            pltpu.VMEM((2, 4, 6, 8, 128), F32),
            pltpu.VMEM((4, 6, 8, 128), F32),
            pltpu.VMEM((6, 8, 8, 128), F32),
            pltpu.VMEM((4, 6, 8, 128), F32),
            pltpu.VMEM((wide, ngy, 8, 128), F32),
            pltpu.VMEM((wide, ngy, 8, 128), F32),
            pltpu.VMEM((2 * ngy + 2, 3, 4, 128), F32),
            pltpu.VMEM((128, 1024), F32),
            pltpu.VMEM((ngy, 8, 128), F32),
            pltpu.VMEM((ngx, 8, 128), F32),
            pltpu.VMEM((ngy, 8, 128), F32),
            pltpu.VMEM((ngx, 8, 128), F32),
            pltpu.VMEM((ngy, 24, 128), F32),
            pltpu.VMEM((ngx, 24, 128), F32),
            dma((5, 9)),
            dma((5, 9)),
            dma((8, max(ngx, ngy))),
            dma((8, max(ngx, ngy))),
            dma((2, wide)),
            dma((2, wide)),
        ],
        compiler_params=pltpu.CompilerParams(
            collective_id=0, has_side_effects=True, vmem_limit_bytes=48 * 1024 * 1024
        ),
    )(modes, directions, locked, perm_class, perm_table, locked_count)


def solution(mesh):
    placed = (
        P(None, "gx", "gy"),
        P(None, "gx", "gy"),
        P(None, "gx", "gy"),
        P("gx", "gy"),
        P(),
        P(),
    )
    return jax.shard_map(
        functools.partial(on_device, mesh.shape["gx"], mesh.shape["gy"]),
        mesh=mesh,
        in_specs=placed,
        out_specs=(P(None, "gx", "gy"), P(None, "gx", "gy"), P(), P()),
        check_vma=False,
    )
```

time: 316 us -> 64.5 us (0.20)
  blocking collectives: 162 us -> 0 us
  starting transfers between devices: 91.7 us -> 0 us
  Pallas kernels: 0 us -> 57.2 us
  waiting for transfers between devices: 23.5 us -> 0 us
  other arithmetic: 14 us -> 0 us
  matrix products: 13.8 us -> 0 us
    psum x3 -> x0, blocking collectives: 134 us -> none  [the longest x1 47.9 us: on_device(): lax.psum(correlation_part, ('gx', 'gy')) / cell_count]
    ppermute x32 -> x0, starting transfers between devices: 91.7 us -> none  [the longest x16 71.1 us: extended(): lax.ppermute(lax.slice_in_dim(block, block.shape[dim] - width, None, axis...]
    pallas_call x0 -> x1, Pallas kernels: none -> 57.2 us  [on_device(): pl.pallas_call(functools.partial(kernel, ngx, ngy), out_shape=(jax.ShapeD...]
    all_gather x2 -> x0, blocking collectives: 28 us -> none  [the longest x1 14.7 us: coarse_solve(): gathered = lax.all_gather(source, 'gy', axis=2, tiled=True)]
    ppermute x32 -> x0, waiting for transfers between devices: 23.5 us -> none  [the longest x16 13.9 us: extended(): lax.ppermute(lax.slice_in_dim(block, block.shape[dim] - width, None, axis...]
    dot_general x16 -> x0, matrix products: 10.7 us -> none  [the longest x3 2.35 us: rayleigh_ritz(): factor = jnp.linalg.cholesky(jnp.dot(raised.T, raised, precision=PRECISE))]
    another operation x20 -> x0, other arithmetic: 9.43 us -> none  [the longest x9 3.13 us: rayleigh_ritz(): factor = jnp.linalg.cholesky(jnp.dot(raised.T, raised, precision=PRECISE))]
    unnamed x19 -> x13, local copies, waits for them, and re-layouts: 0.25 us -> 4.98 us
  transfers between devices with their start and end apart: 32 -> 0, of which waited for: 16 -> 0; matrix products, arithmetic and copies ran while one was open for 2% -> 0% of each run, Pallas kernels for 0% -> 0%
where the time goes in v1:
time: 64.5 us; the launch traced here: 64.1 us
  Pallas kernels  57.2 us (89%)
  local copies, waits for them, and re-layouts  5.63 us (9%)
  between operations  1.33 us (2%)
    pallas_call x1, Pallas kernels, on_device(): pl.pallas_call(functools.partial(kernel, ngx, ngy), out_shape=(jax.ShapeD...  57.2 us
    unnamed x13, local copies, waits for them, and re-layouts  4.98 us

profile of v1, /device:TPU:0, one launch (start us, length us, event | category | flops | bytes accessed | tf_op | source)
XLA Modules:
  0.0 64.1 jit_solution(15193301488890568355)
XLA Ops:
  0.6 0.0 copy-start.4
  1.3 0.0 copy-done.4
  1.3 0.0 copy-start
  1.3 1.0 %copy-done = f32[60,4,512]{2,1,0:T(4,128)S(1)} copy-done((f32[60,4,512]{2,1,0:T(4,128)S(1)}, f32[60,4,512]{2,1,0:T(4,128)}, u32[]{:S(2)}) %copy-start) | copy-done | bytes 491544
  2.3 0.0 copy-start.1
  2.3 0.8 %copy-done.1 = f32[4,4,512]{2,1,0:T(4,128)S(1)} copy-done((f32[4,4,512]{2,1,0:T(4,128)S(1)}, f32[4,4,512]{2,1,0:T(4,128)}, u32[]{:S(2)}) %copy-start.1) | copy-done | bytes 32792
  3.1 0.0 copy-start.2
  3.1 0.8 %copy-done.2 = f32[4,4,512]{2,1,0:T(4,128)S(1)} copy-done((f32[4,4,512]{2,1,0:T(4,128)S(1)}, f32[4,4,512]{2,1,0:T(4,128)}, u32[]{:S(2)}) %copy-start.2) | copy-done | bytes 32792
  3.9 0.0 copy-start.3
  3.9 0.7 %copy-done.3 = s32[4,512]{1,0:T(4,128)S(1)} copy-done((s32[4,512]{1,0:T(4,128)S(1)}, s32[4,512]{1,0:T(4,128)}, u32[]{:S(2)}) %copy-start.3) | copy-done | bytes 8216
  4.6 57.2 %shard_map.93 = (f32[4,4,512]{2,1,0:T(4,128)S(1)}, f32[4,4,512]{2,1,0:T(4,128)S(1)}, f32[4]{0:T(128)S(1)}, f32[60,4]{1,0:T(8,128)S(1)}) custom-call(f32[4,4,512]{2,1,0:T(4,128)S(1)} %copy-done.1, f32[4,4,512]{2,1,0:T(4,128)S(1)} %copy-done.2, f32[60,4,512]{2,1,0:T(4,128)S(1)} %copy-done, s32[4,512]{1,0:T(4,128)S(1)} %copy-done.3, f32[16]{0:T(128)S(1)} %copy-done.4, ...), custom_call_target="tpu_custom_call" | custom-call | tf_op jit(solution)/shard_map/pallas_call | solution.py:533
  61.7 0.7 %copy.10 = f32[60,4]{0,1:T(4,128)} copy(f32[60,4]{1,0:T(8,128)S(1)} %get-tuple-element.7) | data formatting | bytes 1920 | tf_op jit(solution)/shard_map/pallas_call | solution.py:533
  62.4 0.6 copy.15
  63.0 0.6 copy.16
  63.6 0.5 copy.17
Async XLA Ops:
  0.6 0.7 %copy-start.4 = (f32[16]{0:T(128)S(1)}, f32[16]{0:T(128)}, u32[]{:S(2)}) copy-start(f32[16]{0:T(128)} %table_ref.1) | copy-start | bytes 196
  1.3 1.0 %copy-start = (f32[60,4,512]{2,1,0:T(4,128)S(1)}, f32[60,4,512]{2,1,0:T(4,128)}, u32[]{:S(2)}) copy-start(f32[60,4,512]{2,1,0:T(4,128)} %locked_ref.1) | copy-start | bytes 1474564
  2.3 0.8 %copy-start.1 = (f32[4,4,512]{2,1,0:T(4,128)S(1)}, f32[4,4,512]{2,1,0:T(4,128)}, u32[]{:S(2)}) copy-start(f32[4,4,512]{2,1,0:T(4,128)} %modes_ref.1) | copy-start | bytes 98308
  3.1 0.8 %copy-start.2 = (f32[4,4,512]{2,1,0:T(4,128)S(1)}, f32[4,4,512]{2,1,0:T(4,128)}, u32[]{:S(2)}) copy-start(f32[4,4,512]{2,1,0:T(4,128)} %dirs_ref.1) | copy-start | bytes 98308
  3.9 0.7 %copy-start.3 = (s32[4,512]{1,0:T(4,128)S(1)}, s32[4,512]{1,0:T(4,128)}, u32[]{:S(2)}) copy-start(s32[4,512]{1,0:T(4,128)} %class_ref.1) | copy-start | bytes 24580

commit v2 on v1

--- a/solution.py
+++ b/solution.py
@@ -41,6 +41,28 @@
 def face_value(a, b):
     both = (a > 0) & (b > 0)
     return jnp.where(both, 2.0 * a * b / jnp.where(both, a + b, 1.0), 2.0 * (a + b))
+
+
+BF16 = jnp.bfloat16
+
+
+def split(a):
+    high = a.astype(BF16)
+    return high, (a - high.astype(F32)).astype(BF16)
+
+
+def dot_split(a, b_high, b_low, dims):
+    rows = a.shape[0]
+    high = a.astype(BF16).astype(F32)
+    stack = jnp.concatenate([high, a - high], axis=0).astype(BF16)
+    dims = (dims, ((), ()))
+    one = lax.dot_general(stack, b_high, dims, preferred_element_type=F32)
+    two = lax.dot_general(high.astype(BF16), b_low, dims, preferred_element_type=F32)
+    return one[:rows] + (one[rows:] + two)
+
+
+NT = ((1,), (1,))
+NN = ((1,), (0,))
 
 
 class Marks:
@@ -168,10 +190,10 @@
 def kernel(
     ngx,
     ngy,
-    modes_ref,
-    dirs_ref,
-    locked_ref,
-    class_ref,
+    modes_hbm,
+    dirs_hbm,
+    locked_hbm,
+    class_hbm,
     table_ref,
     count_ref,
     new_modes_ref,
@@ -187,6 +209,13 @@
     r2g,
     e2s,
     lst,
+    l_high,
+    l_low,
+    modes_ref,
+    dirs_ref,
+    locked_ref,
+    class_ref,
+    ins,
     by1,
     bx1,
     by2,
@@ -200,6 +229,14 @@
     cs,
     cr,
 ):
+    loads = [
+        pltpu.make_async_copy(src, dst, ins.at[i])
+        for i, (src, dst) in enumerate(
+            [(class_hbm, class_ref), (modes_hbm, modes_ref), (dirs_hbm, dirs_ref), (locked_hbm, locked_ref)]
+        )
+    ]
+    for load in loads:
+        load.start()
     m = Marks()
     gx, gy = lax.axis_index("gx"), lax.axis_index("gy")
     count = ngx * ngy
@@ -308,6 +345,8 @@
 
         return arrive
 
+    for load in loads[:3]:
+        load.wait()
     classes = class_ref[...]
     conduct = jnp.zeros(classes.shape, F32)
     for c in range(table_ref.shape[0]):
@@ -323,6 +362,7 @@
     arrive_k = halo(0, lambda a, b: kh.at[a, b], 2, True)
     arrive_xp = halo(1, lambda a, b: xp.at[:, a, b], 1, False)
 
+    loads[3].wait()
     nl = locked_ref.shape[0]
     for x in range(4):
         for y in range(4):
@@ -334,14 +374,17 @@
     own_x = xp[0, 1:3, 1:5]
     own_p = xp[1, 1:3, 1:5]
     x8 = flat(own_x)
-    mode_dots = fold_locked(m, nt(x8, lst[...]))
+    high, low = split(lst[...])
+    l_high[...] = high
+    l_low[...] = low
+    mode_dots = fold_locked(m, dot_split(x8, l_high[...], l_low[...], NT))
 
     arrive_k()
     arrive_xp()
     own_coef = fine_coef(m, kh[1:5, 1:7])
     image_x = stencil(m, xp[0], own_coef)
     image_x8 = flat(image_x)
-    image_dots = fold_locked(m, nt(image_x8, lst[...]))
+    image_dots = fold_locked(m, dot_split(image_x8, l_high[...], l_low[...], NT))
     first = reduce_start(0, jnp.where(m.half0, image_dots, mode_dots), by1)
 
     wide = fine_coef(m, kh[...])
@@ -367,10 +410,12 @@
     in_use = (j_of < count_ref[0]) & (j_of < nl)
     coupling = jnp.where(in_use, (image_sum - mode_sum * rayleigh) / cells, 0.0)
     coupling = jnp.where(j_of == nl + f_of, rayleigh, coupling)
-    residual = image_x - unflat(nn(spread_locked(m, coupling), lst[...]))
-
-    e0h[1:3, 1:5] = residual * dinv0[1:3, 1:5]
-    arrive_e0 = halo(2, lambda a, b: e0h.at[a, b], 1, False)
+    residual = image_x - unflat(
+        dot_split(spread_locked(m, coupling), l_high[...], l_low[...], NN)
+    )
+
+    e0h[2:4, 2:6] = residual * dinv0[1:3, 1:5]
+    arrive_e0 = halo(2, lambda a, b: e0h.at[a, b], 2, True)
     arrive_c()
     lines = 2 * ngy
     shift = 4.0 / float(lines * lines)
@@ -403,12 +448,13 @@
         faces[y][5] = jnp.where(z4 >= NZ - 4, 0.0, zu)
 
     arrive_e0()
-    r1 = residual - stencil(m, e0h[...], own_coef)
+    e0_wide = e0h[...]
+    r1 = e0_wide[1:5, 1:7] * (wide[0] * (1.0 / OMEGA)) - stencil(m, e0_wide, wide)
     r1 = pair_z(m, pair_y(pair_x(r1)))
-    e1h[2:4, 2:6] = r1 * dinv1[1:3, 1:5]
-    halo(3, lambda a, b: e1h.at[a, b], 2, True)()
-    e1_wide = e1h[...]
-    r2 = r1 - middle_stencil(m, e1_wide[1:5, 1:7], own_mid)
+    e1_near = r1 * dinv1
+    e1h[2:4, 2:6] = e1_near[1:3, 1:5]
+    arrive_e1 = halo(3, lambda a, b: e1h.at[a, b], 2, True)
+    r2 = r1[1:3, 1:5] - middle_stencil(m, e1_near, own_mid)
     r2 = r2[0] + r2[1]
     r2 = jnp.where(m.par0, r2[0] + r2[1], r2[2] + r2[3])
     first_r = gather_start(7, r2g, pair_z2(m, r2))
@@ -442,27 +488,32 @@
     near = e2s[pl.ds(2 * gy, 4)]
     near = jnp.concatenate([near, near], axis=2)
 
+    arrive_e1()
+    e1_wide = e1h[...]
     e1_wide = jnp.stack(
         [jnp.stack([e1_wide[a, b] + near[b // 2, a // 2] for b in range(8)]) for a in range(6)]
     )
     e1 = e1_wide[1:5, 1:7] + e1h[1:5, 1:7] - dinv1 * middle_stencil(m, e1_wide, mid)
-    e0 = e0h[...] + e1
-    precond = e0[1:3, 1:5] + e0h[1:3, 1:5] - dinv0[1:3, 1:5] * stencil(m, e0, own_coef)
+    e0 = e0_wide[1:5, 1:7] + e1
+    precond = e0[1:3, 1:5] + e0_wide[2:4, 2:6] - dinv0[1:3, 1:5] * stencil(m, e0, own_coef)
 
     precond8 = flat(precond)
-    dots = fold_locked(m, nt(precond8, lst[...]))
+    dots = fold_locked(m, dot_split(precond8, l_high[...], l_low[...], NT))
     sums = reduce_end(2, reduce_start(2, dots, by2), by2, bx2)
     corr = jnp.where(in_use, sums / cells, 0.0)
-    corr_ref[...] = corr.T[: corr_ref.shape[0], :ACTIVE]
-    projected8 = precond8 - nn(spread_locked(m, corr), lst[...])
+    corr_ref[...] = corr[:ACTIVE, : corr_ref.shape[1]]
+    projected8 = precond8 - dot_split(spread_locked(m, corr), l_high[...], l_low[...], NN)
     wh[1:3, 1:5] = unflat(projected8)
     halo(4, lambda a, b: wh.at[a, b], 1, False)()
     image_w = stencil(m, wh[...], own_coef)
 
-    trial = jnp.concatenate([x8, projected8, flat(own_p)], axis=0)
-    images = jnp.concatenate([image_x8, flat(image_w), flat(image_p)], axis=0)
-    mass = nt(trial, trial)
-    stiff = 0.5 * (nt(trial, images) + nt(images, trial))
+    fields = jnp.concatenate(
+        [x8, projected8, flat(own_p), image_x8, flat(image_w), flat(image_p)], axis=0
+    )
+    f_high, f_low = split(fields)
+    grams = dot_split(fields, f_high, f_low, NT)
+    mass = grams[:24, :24]
+    stiff = 0.5 * (grams[:24, 24:] + grams[24:, :24])
     both = jnp.concatenate([mass, jnp.zeros((24, 8), F32), stiff, jnp.zeros((24, 72), F32)], axis=1)
     row, col = iota((24, 128), 0), iota((24, 128), 1)
     both = jnp.where((row // 4) % 2 == (col // 4) % 2, both, 0.0)
@@ -508,8 +559,12 @@
     coef = coef + lanes(coef, 4)
     coef = coef + subs(coef, 4)
     coef = jnp.where(m.par0 == ((m.lane // 4) % 2 == 0), coef, 0.0)[:, :24]
-    modes8 = nn(coef, trial)
-    dirs8 = nn(coef[:, 8:], trial[8:])
+    later = jnp.where(iota((8, 24), 1) >= 8, coef, 0.0)
+    pad = jnp.zeros((16, 24), F32)
+    mixed = dot_split(
+        jnp.concatenate([jnp.concatenate([coef, later], axis=0), pad], axis=1), f_high, f_low, NN
+    )
+    modes8, dirs8 = mixed[:8], mixed[8:]
     for x in range(4):
         for y in range(4):
             cut = slice(128 * y, 128 * (y + 1))
@@ -530,26 +585,34 @@
     smem = pl.BlockSpec(memory_space=pltpu.SMEM)
     dma = pltpu.SemaphoreType.DMA
     wide = 2 * REACH + 1
-    return pl.pallas_call(
+    hbm = pl.BlockSpec(memory_space=pltpu.HBM)
+    new_modes, new_dirs, ritz, corr = pl.pallas_call(
         functools.partial(kernel, ngx, ngy),
         out_shape=(
             jax.ShapeDtypeStruct(modes.shape, F32),
             jax.ShapeDtypeStruct(modes.shape, F32),
             jax.ShapeDtypeStruct((ACTIVE,), F32),
-            jax.ShapeDtypeStruct((locked.shape[0], ACTIVE), F32),
+            jax.ShapeDtypeStruct((ACTIVE, locked.shape[0]), F32),
         ),
-        in_specs=[vmem, vmem, vmem, vmem, smem, smem],
+        in_specs=[hbm, hbm, hbm, hbm, smem, smem],
         out_specs=(vmem, vmem, smem, vmem),
         scratch_shapes=[
             pltpu.VMEM((6, 8, 8, 128), F32),
             pltpu.VMEM((2, 4, 6, 8, 128), F32),
-            pltpu.VMEM((4, 6, 8, 128), F32),
+            pltpu.VMEM((6, 8, 8, 128), F32),
             pltpu.VMEM((6, 8, 8, 128), F32),
             pltpu.VMEM((4, 6, 8, 128), F32),
             pltpu.VMEM((wide, ngy, 8, 128), F32),
             pltpu.VMEM((wide, ngy, 8, 128), F32),
             pltpu.VMEM((2 * ngy + 2, 3, 4, 128), F32),
             pltpu.VMEM((128, 1024), F32),
+            pltpu.VMEM((128, 1024), BF16),
+            pltpu.VMEM((128, 1024), BF16),
+            pltpu.VMEM(modes.shape, F32),
+            pltpu.VMEM(directions.shape, F32),
+            pltpu.VMEM(locked.shape, F32),
+            pltpu.VMEM(perm_class.shape, jnp.int32),
+            dma((4,)),
             pltpu.VMEM((ngy, 8, 128), F32),
             pltpu.VMEM((ngx, 8, 128), F32),
             pltpu.VMEM((ngy, 8, 128), F32),
@@ -564,9 +627,10 @@
             dma((2, wide)),
         ],
         compiler_params=pltpu.CompilerParams(
-            collective_id=0, has_side_effects=True, vmem_limit_bytes=48 * 1024 * 1024
+            collective_id=0, has_side_effects=True, vmem_limit_bytes=64 * 1024 * 1024 - 65536
         ),
     )(modes, directions, locked, perm_class, perm_table, locked_count)
+    return new_modes, new_dirs, ritz, corr.T
 
 
 def solution(mesh):

time: 64.5 us -> 58.4 us (0.905)
  Pallas kernels: 57.2 us -> 53.8 us
  local copies, waits for them, and re-layouts: 5.63 us -> 3.14 us
    pallas_call x1, Pallas kernels: 57.2 us -> 53.8 us  [on_device(): pl.pallas_call(functools.partial(kernel, ngx, ngy), out_shape=(jax.ShapeD...]
    unnamed x13 -> x10, local copies, waits for them, and re-layouts: 4.98 us -> 3.14 us
    pallas_call x1 -> x0, local copies, waits for them, and re-layouts: 0.65 us -> none  [on_device(): pl.pallas_call(functools.partial(kernel, ngx, ngy), out_shape=(jax.ShapeD...]
where the time goes in v2:
time: 58.4 us; the launch traced here: 58.2 us
  Pallas kernels  53.8 us (92%)
  local copies, waits for them, and re-layouts  3.14 us (5%)
  between operations  1.3 us (2%)
    pallas_call x1, Pallas kernels, on_device(): pl.pallas_call(functools.partial(kernel, ngx, ngy), out_shape=(jax.ShapeD...  53.8 us
    unnamed x10, local copies, waits for them, and re-layouts  3.14 us

profile of v2, /device:TPU:0, one launch (start us, length us, event | category | flops | bytes accessed | tf_op | source)
XLA Modules:
  0.0 58.2 jit_solution(9861279643798617617)
XLA Ops:
  1.3 53.8 %shard_map.93 = (f32[4,4,512]{2,1,0:T(4,128)}, f32[4,4,512]{2,1,0:T(4,128)}, f32[4]{0:T(128)}, f32[4,60]{1,0:T(4,128)}) custom-call(f32[4,4,512]{2,1,0:T(4,128)} %modes_hbm.1, f32[4,4,512]{2,1,0:T(4,128)} %dirs_hbm.1, f32[60,4,512]{2,1,0:T(4,128)} %locked_hbm.1, s32[4,512]{1,0:T(4,128)} %class_hbm.1, f32[16]{0:T(128)} %table_ref.1, s32[1]{0:T(128)S(6)} %copy.14.count_ref), custom_call_target="tpu_custom_call" | custom-call | tf_op jit(solution)/shard_map/pallas_call | solution.py:589
  55.0 0.0 copy-start
  55.1 1.4 %copy.15 = f32[4,4,512]{2,1,0:T(4,128)} copy(f32[4,4,512]{2,1,0:T(4,128)} %get-tuple-element.16) | data formatting | bytes 65536
  56.4 0.0 copy-done
  56.4 0.0 copy-start.2
  56.4 0.0 copy-start.1
  56.4 0.6 %copy.16 = f32[4,4,512]{2,1,0:T(4,128)} copy(f32[4,4,512]{2,1,0:T(4,128)S(1)} %copy-done) | data formatting | bytes 65536
  57.1 0.0 copy-done.2
  57.1 0.5 copy.17
  57.6 0.0 copy-done.1
  57.6 0.6 copy.18
Async XLA Ops:
  55.0 1.4 %copy-start = (f32[4,4,512]{2,1,0:T(4,128)S(1)}, f32[4,4,512]{2,1,0:T(4,128)}, u32[]{:S(2)}) copy-start(f32[4,4,512]{2,1,0:T(4,128)} %get-tuple-element.17) | copy-start | bytes 98308
  56.4 0.7 %copy-start.2 = (f32[4]{0:T(128)S(1)}, f32[4]{0:T(128)}, u32[]{:S(2)}) copy-start(f32[4]{0:T(128)} %get-tuple-element.18) | copy-start | bytes 52
  56.4 1.2 %copy-start.1 = (f32[4,60]{1,0:T(4,128)S(1)}, f32[4,60]{1,0:T(4,128)}, u32[]{:S(2)}) copy-start(f32[4,60]{1,0:T(4,128)} %get-tuple-element.11) | copy-start | bytes 2884

commit v3 on v2

--- a/solution.py
+++ b/solution.py
@@ -196,9 +196,8 @@
     class_hbm,
     table_ref,
     count_ref,
-    new_modes_ref,
-    new_dirs_ref,
-    ritz_ref,
+    sums_ref,
+    trial_ref,
     corr_ref,
     kh,
     xp,
@@ -247,16 +246,22 @@
         buf[...] = jnp.zeros(buf.shape, F32)
 
     barrier = pltpu.get_barrier_semaphore()
-    me = gx * ngy + gy
-
-    def greet(i, carry):
-        other = lax.rem(me + i, count)
-        pl.semaphore_signal(
-            barrier, inc=1, device_id=(other // ngy, lax.rem(other, ngy)), device_id_type=pl.DeviceIdType.MESH
-        )
-        return carry
-
-    lax.fori_loop(1, count, greet, 0)
+
+    def greet(tx, ty):
+        pl.semaphore_signal(barrier, inc=1, device_id=(tx, ty), device_id_type=pl.DeviceIdType.MESH)
+
+    for i in range(1, ngx):
+        greet(lax.rem(gx + i, ngx), gy)
+    for i in range(1, ngy):
+        greet(gx, lax.rem(gy + i, ngy))
+    for dx in (-1, 1):
+        for dy in (-1, 1):
+            pl.when(
+                (gx + dx >= 0) & (gx + dx < ngx) & (gy + dy >= 0) & (gy + dy < ngy)
+            )(functools.partial(greet, gx + dx, gy + dy))
+    beside_x = jnp.where(gx > 0, 1, 0) + jnp.where(gx < ngx - 1, 1, 0)
+    beside_y = jnp.where(gy > 0, 1, 0) + jnp.where(gy < ngy - 1, 1, 0)
+    greeted = ngx + ngy - 2 + beside_x * beside_y
 
     def remote(src, dst, send, recv, tx, ty):
         return pltpu.make_async_remote_copy(
@@ -315,10 +320,13 @@
         bufy[gy] = val
         return share(slot, bufy, gy, ngy, "gy", lambda b, i: b.at[i])
 
-    def reduce_end(slot, first, bufy, bufx):
+    def reduce_next(slot, first, bufy, bufx):
         first()
         bufx[gx] = total([bufy[j] for j in range(ngy)])
-        share(slot + 1, bufx, gx, ngx, "gx", lambda b, i: b.at[i])()
+        return share(slot + 1, bufx, gx, ngx, "gx", lambda b, i: b.at[i])
+
+    def reduce_end(slot, first, bufy, bufx):
+        reduce_next(slot, first, bufy, bufx)()
         return total([bufx[j] for j in range(ngx)])
 
     def gather_start(slot, buf, val):
@@ -358,7 +366,7 @@
             kh[2 + x // 2, 2 + y, rows, :] = jnp.broadcast_to(conduct[x : x + 1, cut], (4, 128))
             xp[0, 1 + x // 2, 1 + y, rows, :] = modes_ref[:, x, cut]
             xp[1, 1 + x // 2, 1 + y, rows, :] = dirs_ref[:, x, cut]
-    pl.semaphore_wait(barrier, count - 1)
+    pl.semaphore_wait(barrier, greeted)
     arrive_k = halo(0, lambda a, b: kh.at[a, b], 2, True)
     arrive_xp = halo(1, lambda a, b: xp.at[:, a, b], 1, False)
 
@@ -390,14 +398,14 @@
     wide = fine_coef(m, kh[...])
     in_grid = kh[1:5, 1:7] > 0
     dinv0 = inverse(wide[0], in_grid)
+    second = reduce_next(0, first, by1, bx1)
     mid = middle_coef(m, wide)
     dinv1 = inverse(mid[0], in_grid)
     own_mid = [c[1:3, 1:5] for c in mid]
     first_c = gather_start(6, ccg, coarse_pack(m, own_mid))
     image_p = stencil(m, xp[1], own_coef)
-
-    sums = reduce_end(0, first, by1, bx1)
-    arrive_c = gather_next(0, first_c, ccg)
+    second()
+    sums = total([bx1[j] for j in range(ngx)])
 
     f_of = m.sub % 4
     top = jnp.sum(jnp.where(m.lane == nl + f_of, sums, 0.0), axis=1, keepdims=True)
@@ -416,6 +424,18 @@
 
     e0h[2:4, 2:6] = residual * dinv0[1:3, 1:5]
     arrive_e0 = halo(2, lambda a, b: e0h.at[a, b], 2, True)
+    arrive_c = gather_next(0, first_c, ccg)
+    arrive_e0()
+    e0_wide = e0h[...]
+    r1 = e0_wide[1:5, 1:7] * (wide[0] * (1.0 / OMEGA)) - stencil(m, e0_wide, wide)
+    r1 = pair_z(m, pair_y(pair_x(r1)))
+    e1_near = r1 * dinv1
+    e1h[2:4, 2:6] = e1_near[1:3, 1:5]
+    arrive_e1 = halo(3, lambda a, b: e1h.at[a, b], 2, True)
+    r2 = r1[1:3, 1:5] - middle_stencil(m, e1_near, own_mid)
+    r2 = r2[0] + r2[1]
+    r2 = jnp.where(m.par0, r2[0] + r2[1], r2[2] + r2[3])
+    first_r = gather_start(7, r2g, pair_z2(m, r2))
     arrive_c()
     lines = 2 * ngy
     shift = 4.0 / float(lines * lines)
@@ -447,17 +467,6 @@
         faces[y][4] = jnp.where(z4 < 4, 0.0, zl)
         faces[y][5] = jnp.where(z4 >= NZ - 4, 0.0, zu)
 
-    arrive_e0()
-    e0_wide = e0h[...]
-    r1 = e0_wide[1:5, 1:7] * (wide[0] * (1.0 / OMEGA)) - stencil(m, e0_wide, wide)
-    r1 = pair_z(m, pair_y(pair_x(r1)))
-    e1_near = r1 * dinv1
-    e1h[2:4, 2:6] = e1_near[1:3, 1:5]
-    arrive_e1 = halo(3, lambda a, b: e1h.at[a, b], 2, True)
-    r2 = r1[1:3, 1:5] - middle_stencil(m, e1_near, own_mid)
-    r2 = r2[0] + r2[1]
-    r2 = jnp.where(m.par0, r2[0] + r2[1], r2[2] + r2[3])
-    first_r = gather_start(7, r2g, pair_z2(m, r2))
     gather_next(1, first_r, r2g)()
 
     source = [r2g[:, y // 2, 4 * (y % 2) : 4 * (y % 2) + 4] for y in range(lines)]
@@ -519,8 +528,34 @@
     both = jnp.where((row // 4) % 2 == (col // 4) % 2, both, 0.0)
     both = both + jnp.concatenate([subs(both[8 * i : 8 * i + 8], 4) for i in range(3)], axis=0)
     both = both + lanes(both, -4)
-    sums = reduce_end(4, reduce_start(4, both, by3), by3, bx3) / cells
-
+    trial_ref[...] = fields[:24]
+    sums_ref[...] = reduce_end(4, reduce_start(4, both, by3), by3, bx3) / cells
+
+    for copy, to in pending:
+        if to is None:
+            copy.wait_send()
+        else:
+            pl.when(to)(copy.wait_send)
+
+
+def finish(
+    sums_hbm, trial_hbm, corr_hbm, new_modes_hbm, new_dirs_hbm, ritz_ref, corr_out,
+    sums_ref, trial_ref, corr_ref, new_modes_ref, new_dirs_ref, sems,
+):
+    loads = [
+        pltpu.make_async_copy(sums_hbm, sums_ref, sems.at[0]),
+        pltpu.make_async_copy(trial_hbm, trial_ref, sems.at[1]),
+        pltpu.make_async_copy(corr_hbm, corr_ref, sems.at[2]),
+    ]
+    for load in loads:
+        load.start()
+    m = Marks()
+    row, col = iota((24, 128), 0), iota((24, 128), 1)
+    for load in loads:
+        load.wait()
+    store_corr = pltpu.make_async_copy(corr_ref, corr_out, sems.at[3])
+    store_corr.start()
+    sums = sums_ref[...]
     real = row % 8 < 4
     table = jnp.where(real & (col < 64) & (col % 8 < 4), sums, 0.0)
     table = jnp.where(real & (col == row + 64), 1.0, table)
@@ -559,11 +594,9 @@
     coef = coef + lanes(coef, 4)
     coef = coef + subs(coef, 4)
     coef = jnp.where(m.par0 == ((m.lane // 4) % 2 == 0), coef, 0.0)[:, :24]
+    f_high, f_low = split(trial_ref[...])
     later = jnp.where(iota((8, 24), 1) >= 8, coef, 0.0)
-    pad = jnp.zeros((16, 24), F32)
-    mixed = dot_split(
-        jnp.concatenate([jnp.concatenate([coef, later], axis=0), pad], axis=1), f_high, f_low, NN
-    )
+    mixed = dot_split(jnp.concatenate([coef, later], axis=0), f_high, f_low, NN)
     modes8, dirs8 = mixed[:8], mixed[8:]
     for x in range(4):
         for y in range(4):
@@ -572,12 +605,14 @@
             rows = slice(4 * (x % 2), 4 * (x % 2) + 4)
             new_modes_ref[:, x, cut] = modes8[rows, frm]
             new_dirs_ref[:, x, cut] = dirs8[rows, frm]
-
-    for copy, to in pending:
-        if to is None:
-            copy.wait_send()
-        else:
-            pl.when(to)(copy.wait_send)
+    stores = [
+        pltpu.make_async_copy(new_modes_ref, new_modes_hbm, sems.at[4]),
+        pltpu.make_async_copy(new_dirs_ref, new_dirs_hbm, sems.at[5]),
+    ]
+    for store in stores:
+        store.start()
+    for store in stores + [store_corr]:
+        store.wait()
 
 
 def on_device(ngx, ngy, modes, directions, locked, perm_class, perm_table, locked_count):
@@ -586,16 +621,16 @@
     dma = pltpu.SemaphoreType.DMA
     wide = 2 * REACH + 1
     hbm = pl.BlockSpec(memory_space=pltpu.HBM)
-    new_modes, new_dirs, ritz, corr = pl.pallas_call(
+    limit = 64 * 1024 * 1024 - 65536
+    sums, trial, corr = pl.pallas_call(
         functools.partial(kernel, ngx, ngy),
         out_shape=(
-            jax.ShapeDtypeStruct(modes.shape, F32),
-            jax.ShapeDtypeStruct(modes.shape, F32),
-            jax.ShapeDtypeStruct((ACTIVE,), F32),
+            jax.ShapeDtypeStruct((24, 128), F32),
+            jax.ShapeDtypeStruct((24, 1024), F32),
             jax.ShapeDtypeStruct((ACTIVE, locked.shape[0]), F32),
         ),
         in_specs=[hbm, hbm, hbm, hbm, smem, smem],
-        out_specs=(vmem, vmem, smem, vmem),
+        out_specs=(vmem, vmem, vmem),
         scratch_shapes=[
             pltpu.VMEM((6, 8, 8, 128), F32),
             pltpu.VMEM((2, 4, 6, 8, 128), F32),
@@ -627,9 +662,29 @@
             dma((2, wide)),
         ],
         compiler_params=pltpu.CompilerParams(
-            collective_id=0, has_side_effects=True, vmem_limit_bytes=64 * 1024 * 1024 - 65536
+            collective_id=0, has_side_effects=True, vmem_limit_bytes=limit
         ),
     )(modes, directions, locked, perm_class, perm_table, locked_count)
+    new_modes, new_dirs, ritz, corr = pl.pallas_call(
+        finish,
+        out_shape=(
+            jax.ShapeDtypeStruct(modes.shape, F32),
+            jax.ShapeDtypeStruct(modes.shape, F32),
+            jax.ShapeDtypeStruct((ACTIVE,), F32),
+            jax.ShapeDtypeStruct(corr.shape, F32),
+        ),
+        in_specs=[hbm, hbm, hbm],
+        out_specs=(hbm, hbm, smem, hbm),
+        scratch_shapes=[
+            pltpu.VMEM(sums.shape, F32),
+            pltpu.VMEM(trial.shape, F32),
+            pltpu.VMEM(corr.shape, F32),
+            pltpu.VMEM(modes.shape, F32),
+            pltpu.VMEM(modes.shape, F32),
+            dma((6,)),
+        ],
+        compiler_params=pltpu.CompilerParams(vmem_limit_bytes=limit),
+    )(sums, trial, corr)
     return new_modes, new_dirs, ritz, corr.T
 
 

time: 58.4 us -> 55.4 us (0.949)
  local copies, waits for them, and re-layouts: 3.14 us -> 0 us
    pallas_call x0 -> x1, Pallas kernels: none -> 4.72 us  [on_device(): pl.pallas_call(finish, out_shape=(jax.ShapeDtypeStruct(modes.shape, F32),...]
    pallas_call x1, Pallas kernels: 53.8 us -> 49.1 us  [on_device(): pl.pallas_call(functools.partial(kernel, ngx, ngy), out_shape=(jax.ShapeD...]
    unnamed x10 -> x0, local copies, waits for them, and re-layouts: 3.14 us -> none
where the time goes in v3:
time: 55.4 us; the launch traced here: 55.1 us
  Pallas kernels  53.8 us (97%)
  between operations  1.29 us (2%)
    pallas_call x1, Pallas kernels, on_device(): pl.pallas_call(functools.partial(kernel, ngx, ngy), out_shape=(jax.ShapeD...  49.1 us
    pallas_call x1, Pallas kernels, on_device(): pl.pallas_call(finish, out_shape=(jax.ShapeDtypeStruct(modes.shape, F32),...  4.72 us

profile of v3, /device:TPU:0, one launch (start us, length us, event | category | flops | bytes accessed | tf_op | source)
XLA Modules:
  0.0 55.1 jit_solution(401816872220916450)
XLA Ops:
  1.3 49.1 %shard_map.93 = (f32[24,128]{1,0:T(8,128)}, f32[24,1024]{1,0:T(8,128)}, f32[4,60]{1,0:T(4,128)}) custom-call(f32[4,4,512]{2,1,0:T(4,128)} %modes_hbm.1, f32[4,4,512]{2,1,0:T(4,128)} %dirs_hbm.1, f32[60,4,512]{2,1,0:T(4,128)} %locked_hbm.1, s32[4,512]{1,0:T(4,128)} %class_hbm.1, f32[16]{0:T(128)} %table_ref.1, s32[1]{0:T(128)S(6)} %copy.10.count_ref), custom_call_target="tpu_custom_call" | custom-call | tf_op jit(solution)/shard_map/pallas_call | solution.py:625
  50.4 4.7 %shard_map.94 = (f32[4,4,512]{2,1,0:T(4,128)}, f32[4,4,512]{2,1,0:T(4,128)}, f32[4]{0:T(128)}, f32[4,60]{1,0:T(4,128)}) custom-call(f32[24,128]{1,0:T(8,128)} %get-tuple-element.11.sums_hbm, f32[24,1024]{1,0:T(8,128)} %get-tuple-element.12.trial_hbm, f32[4,60]{1,0:T(4,128)} %get-tuple-element.13.corr_hbm), custom_call_target="tpu_custom_call" | custom-call | tf_op jit(solution)/shard_map/pallas_call | solution.py:668

commit v4 on v3

--- a/solution.py
+++ b/solution.py
@@ -203,10 +203,15 @@
     xp,
     e0h,
     e1h,
-    wh,
     ccg,
     r2g,
     e2s,
+    lxlow,
+    lxhigh,
+    lylow,
+    lyhigh,
+    lysend,
+    al,
     lst,
     l_high,
     l_low,
@@ -242,7 +247,7 @@
     cells = float(4 * 512 * count)
     pending = []
 
-    for buf in (kh, xp, e0h, e1h, wh, ccg, r2g, e2s):
+    for buf in (kh, xp, e0h, e1h, ccg, r2g, e2s, lxlow, lxhigh, lylow, lyhigh):
         buf[...] = jnp.zeros(buf.shape, F32)
 
     barrier = pltpu.get_barrier_semaphore()
@@ -379,6 +384,30 @@
             lst[pl.ds(64 * (x % 2), nl), to] = locked_ref[:, x, cut]
             lst[pl.ds(64 * (x % 2) + nl, 4), to] = modes_ref[:, x, cut]
 
+    def tile(x, y, par):
+        return lst[64 * par : 64 * par + 64, 128 * (4 * x + y) : 128 * (4 * x + y) + 128]
+
+    def column(x, y):
+        return lst[:, 128 * (4 * x + y) : 128 * (4 * x + y) + 128]
+
+    wide_lane = iota((128, 128), 1) < 64
+    lysend[0] = jnp.where(wide_lane, lanes(column(0, 3), 64), column(1, 3))
+    lysend[1] = jnp.where(wide_lane, column(0, 0), lanes(column(1, 0), 64))
+    locked_copies = []
+    for n, (src, dst, dx, dy) in enumerate(
+        [
+            (lst.at[pl.ds(64, 64), pl.ds(512, 512)], lxlow, 1, 0),
+            (lst.at[pl.ds(0, 64), pl.ds(0, 512)], lxhigh, -1, 0),
+            (lysend.at[0], lylow, 0, 1),
+            (lysend.at[1], lyhigh, 0, -1),
+        ]
+    ):
+        copy = remote(src, dst, hs.at[4, n], hr.at[4, n], gx + dx, gy + dy)
+        to, frm = inside(gx + dx, gy + dy), inside(gx - dx, gy - dy)
+        pl.when(to)(copy.start)
+        pending.append((copy, to))
+        locked_copies.append((copy, frm))
+
     own_x = xp[0, 1:3, 1:5]
     own_p = xp[1, 1:3, 1:5]
     x8 = flat(own_x)
@@ -425,6 +454,34 @@
     e0h[2:4, 2:6] = residual * dinv0[1:3, 1:5]
     arrive_e0 = halo(2, lambda a, b: e0h.at[a, b], 2, True)
     arrive_c = gather_next(0, first_c, ccg)
+    for copy, frm in locked_copies:
+        pl.when(frm)(copy.wait_recv)
+    low64 = iota((64, 128), 1) < 64
+    z_row = iota((1, 128), 1) % NZ
+    for x in range(2):
+        for par in range(2):
+            rows = slice(64 * par, 64 * par + 64)
+            flips = [lanes(tile(x, y, par), 64) for y in range(4)]
+            before = lylow[rows] if x == 0 else lanes(lylow[rows], 64)
+            after = lyhigh[rows] if x == 1 else lanes(lyhigh[rows], 64)
+            flips = [before] + flips + [after]
+            for y in range(4):
+                u = tile(x, y, par)
+                cut = slice(128 * y, 128 * y + 128)
+                if par:
+                    xl = tile(x, y, 0)
+                    xu = tile(1, y, 0) if x == 0 else lxhigh[:, cut]
+                else:
+                    xl = tile(0, y, 1) if x == 1 else lxlow[:, cut]
+                    xu = tile(x, y, 1)
+                yl = jnp.where(low64, flips[y], flips[y + 1])
+                yu = jnp.where(low64, flips[y + 1], flips[y + 2])
+                c = [k[x, y, 4 * par : 4 * par + 1] for k in own_coef]
+                near = c[1] * xl + c[2] * xu + c[3] * yl + c[4] * yu
+                near = near + jnp.where(z_row == 0, 0.0, c[5]) * lanes(u, 1)
+                near = near + jnp.where(z_row == NZ - 1, 0.0, c[6]) * lanes(u, -1)
+                al[rows, 128 * (4 * x + y) : 128 * (4 * x + y) + 128] = c[0] * u - near
+
     arrive_e0()
     e0_wide = e0h[...]
     r1 = e0_wide[1:5, 1:7] * (wide[0] * (1.0 / OMEGA)) - stencil(m, e0_wide, wide)
@@ -467,7 +524,13 @@
         faces[y][4] = jnp.where(z4 < 4, 0.0, zl)
         faces[y][5] = jnp.where(z4 >= NZ - 4, 0.0, zu)
 
-    gather_next(1, first_r, r2g)()
+    arrive_r = gather_next(1, first_r, r2g)
+    square = []
+    for left in (lst[...], al[...]):
+        whole = dot_split(left, l_high[...], l_low[...], NT)
+        square.append(whole[:64, :64] + whole[64:, 64:])
+    first_s = reduce_start(4, jnp.concatenate(square, axis=1), by3)
+    arrive_r()
 
     source = [r2g[:, y // 2, 4 * (y % 2) : 4 * (y % 2) + 4] for y in range(lines)]
     held = []
@@ -504,32 +567,63 @@
     )
     e1 = e1_wide[1:5, 1:7] + e1h[1:5, 1:7] - dinv1 * middle_stencil(m, e1_wide, mid)
     e0 = e0_wide[1:5, 1:7] + e1
-    precond = e0[1:3, 1:5] + e0_wide[2:4, 2:6] - dinv0[1:3, 1:5] * stencil(m, e0, own_coef)
-
+    edge_y, edge_x = jnp.zeros((4, 1, 8, 128), F32), jnp.zeros((1, 8, 8, 128), F32)
+    e0_rim = jnp.concatenate([edge_y, e0, edge_y], axis=1)
+    e0_rim = jnp.concatenate([edge_x, e0_rim, edge_x], axis=0)
+    precond_wide = e0 + e0_wide[1:5, 1:7] - dinv0 * stencil(m, e0_rim, wide)
+    precond = precond_wide[1:3, 1:5]
+    image_w = stencil(m, precond_wide, own_coef)
     precond8 = flat(precond)
-    dots = fold_locked(m, dot_split(precond8, l_high[...], l_low[...], NT))
-    sums = reduce_end(2, reduce_start(2, dots, by2), by2, bx2)
-    corr = jnp.where(in_use, sums / cells, 0.0)
+    fields = jnp.concatenate([precond8, flat(own_p), flat(image_w), flat(image_p)], axis=0)
+    with_locked = dot_split(fields, l_high[...], l_low[...], NT)
+    f_pc, f_p, f_apc, f_ap = [fold_locked(m, with_locked[8 * i : 8 * i + 8]) for i in range(4)]
+    cross = jnp.where(m.par0, jnp.where(m.half0, f_pc, f_apc), jnp.where(m.half0, f_p, f_ap))
+    f_high, f_low = split(fields[:16])
+    among = dot_split(fields, f_high, f_low, NT)
+    row, col = iota((32, 16), 0), iota((32, 16), 1)
+    among = jnp.where((row // 4) % 2 == (col // 4) % 2, among, 0.0)
+    among = jnp.concatenate(
+        [among[:16], jnp.zeros((16, 48), F32), among[16:], jnp.zeros((16, 48), F32)], axis=1
+    )
+    among = [among[:8], among[8:]]
+    among = [u + subs(u, 4) for u in among]
+    own = jnp.where(m.par0, among[0], among[1])
+    own = own + lanes(own, -4)
+    first = reduce_start(2, jnp.concatenate([cross, own], axis=0), by2)
+    second_s = reduce_next(4, first_s, by3, bx3)
+    late = reduce_end(2, first, by2, bx2) / cells
+    cross, own = late[:8], late[8:]
+    corr = jnp.where(in_use & m.half0 & m.par0, cross, 0.0)
     corr_ref[...] = corr[:ACTIVE, : corr_ref.shape[1]]
-    projected8 = precond8 - dot_split(spread_locked(m, corr), l_high[...], l_low[...], NN)
-    wh[1:3, 1:5] = unflat(projected8)
-    halo(4, lambda a, b: wh.at[a, b], 1, False)()
-    image_w = stencil(m, wh[...], own_coef)
-
-    fields = jnp.concatenate(
-        [x8, projected8, flat(own_p), image_x8, flat(image_w), flat(image_p)], axis=0
+    twice = corr + subs(corr, 4)
+    twice = twice + lanes(twice, 64)
+    projected8 = precond8 - dot_split(spread_locked(m, twice), l_high[...], l_low[...], NN)
+    trial_ref[...] = jnp.concatenate([x8, projected8, flat(own_p)], axis=0)
+    second_s()
+    inner = total([bx3[j] for j in range(ngx)]) / cells
+
+    zero = jnp.zeros((8, 64), F32)
+    low8 = iota((8, 64), 0) < 4
+    spot = iota((8, 64), 1) == nl + iota((8, 64), 0)
+    combine = jnp.concatenate([jnp.where(low8 & spot, 1.0, 0.0), -corr[:, :64], zero], axis=0)
+    grams = []
+    for i in range(2):
+        cut = slice(64 * i, 64 * i + 64)
+        part = cross[:, cut]
+        direct = jnp.concatenate(
+            [zero, jnp.where(low8, part, 0.0), jnp.where(low8, subs(part, 4), 0.0)], axis=0
+        )
+        gram = nt(nn(combine, inner[:, cut]) + direct, combine) + nt(combine, direct)
+        some = own[:, 64 * i : 64 * i + 16]
+        some = jnp.where((iota((8, 16), 1) // 4) % 2 == 0, some, 0.0)
+        low16 = iota((8, 16), 0) < 4
+        some = jnp.concatenate(
+            [jnp.zeros((8, 16), F32), jnp.where(low16, some, 0.0), jnp.where(low16, subs(some, 4), 0.0)], axis=0
+        )
+        grams.append(gram + jnp.concatenate([jnp.zeros((24, 8), F32), some], axis=1))
+    sums_ref[...] = jnp.concatenate(
+        [grams[0], jnp.zeros((24, 8), F32), grams[1], jnp.zeros((24, 72), F32)], axis=1
     )
-    f_high, f_low = split(fields)
-    grams = dot_split(fields, f_high, f_low, NT)
-    mass = grams[:24, :24]
-    stiff = 0.5 * (grams[:24, 24:] + grams[24:, :24])
-    both = jnp.concatenate([mass, jnp.zeros((24, 8), F32), stiff, jnp.zeros((24, 72), F32)], axis=1)
-    row, col = iota((24, 128), 0), iota((24, 128), 1)
-    both = jnp.where((row // 4) % 2 == (col // 4) % 2, both, 0.0)
-    both = both + jnp.concatenate([subs(both[8 * i : 8 * i + 8], 4) for i in range(3)], axis=0)
-    both = both + lanes(both, -4)
-    trial_ref[...] = fields[:24]
-    sums_ref[...] = reduce_end(4, reduce_start(4, both, by3), by3, bx3) / cells
 
     for copy, to in pending:
         if to is None:
@@ -636,10 +730,15 @@
             pltpu.VMEM((2, 4, 6, 8, 128), F32),
             pltpu.VMEM((6, 8, 8, 128), F32),
             pltpu.VMEM((6, 8, 8, 128), F32),
-            pltpu.VMEM((4, 6, 8, 128), F32),
             pltpu.VMEM((wide, ngy, 8, 128), F32),
             pltpu.VMEM((wide, ngy, 8, 128), F32),
             pltpu.VMEM((2 * ngy + 2, 3, 4, 128), F32),
+            pltpu.VMEM((64, 512), F32),
+            pltpu.VMEM((64, 512), F32),
+            pltpu.VMEM((128, 128), F32),
+            pltpu.VMEM((128, 128), F32),
+            pltpu.VMEM((2, 128, 128), F32),
+            pltpu.VMEM((128, 1024), F32),
             pltpu.VMEM((128, 1024), F32),
             pltpu.VMEM((128, 1024), BF16),
             pltpu.VMEM((128, 1024), BF16),
@@ -650,10 +749,10 @@
             dma((4,)),
             pltpu.VMEM((ngy, 8, 128), F32),
             pltpu.VMEM((ngx, 8, 128), F32),
-            pltpu.VMEM((ngy, 8, 128), F32),
-            pltpu.VMEM((ngx, 8, 128), F32),
-            pltpu.VMEM((ngy, 24, 128), F32),
-            pltpu.VMEM((ngx, 24, 128), F32),
+            pltpu.VMEM((ngy, 16, 128), F32),
+            pltpu.VMEM((ngx, 16, 128), F32),
+            pltpu.VMEM((ngy, 64, 128), F32),
+            pltpu.VMEM((ngx, 64, 128), F32),
             dma((5, 9)),
             dma((5, 9)),
             dma((8, max(ngx, ngy))),

time: 55.4 us -> 46.9 us (0.85)
  Pallas kernels: 53.8 us -> 45.3 us
    pallas_call x1, Pallas kernels: 49.1 us -> 40.6 us  [on_device(): pl.pallas_call(functools.partial(kernel, ngx, ngy), out_shape=(jax.ShapeD...]
where the time goes in v4:
time: 46.9 us; the launch traced here: 46.6 us
  Pallas kernels  45.3 us (97%)
  between operations  1.29 us (3%)
    pallas_call x1, Pallas kernels, on_device(): pl.pallas_call(functools.partial(kernel, ngx, ngy), out_shape=(jax.ShapeD...  40.6 us
    pallas_call x1, Pallas kernels, on_device(): pl.pallas_call(finish, out_shape=(jax.ShapeDtypeStruct(modes.shape, F32),...  4.72 us

profile of v4, /device:TPU:0, one launch (start us, length us, event | category | flops | bytes accessed | tf_op | source)
XLA Modules:
  0.0 46.6 jit_solution(12465736384072562660)
XLA Ops:
  1.3 40.6 %shard_map.93 = (f32[24,128]{1,0:T(8,128)}, f32[24,1024]{1,0:T(8,128)}, f32[4,60]{1,0:T(4,128)}) custom-call(f32[4,4,512]{2,1,0:T(4,128)} %modes_hbm.1, f32[4,4,512]{2,1,0:T(4,128)} %dirs_hbm.1, f32[60,4,512]{2,1,0:T(4,128)} %locked_hbm.1, s32[4,512]{1,0:T(4,128)} %class_hbm.1, f32[16]{0:T(128)} %table_ref.1, s32[1]{0:T(128)S(6)} %copy.10.count_ref), custom_call_target="tpu_custom_call" | custom-call | tf_op jit(solution)/shard_map/pallas_call | solution.py:719
  41.9 4.7 %shard_map.94 = (f32[4,4,512]{2,1,0:T(4,128)}, f32[4,4,512]{2,1,0:T(4,128)}, f32[4]{0:T(128)}, f32[4,60]{1,0:T(4,128)}) custom-call(f32[24,128]{1,0:T(8,128)} %get-tuple-element.11.sums_hbm, f32[24,1024]{1,0:T(8,128)} %get-tuple-element.12.trial_hbm, f32[4,60]{1,0:T(4,128)} %get-tuple-element.13.corr_hbm), custom_call_target="tpu_custom_call" | custom-call | tf_op jit(solution)/shard_map/pallas_call | solution.py:767

commit v5 on v4

--- a/solution.py
+++ b/solution.py
@@ -221,7 +221,6 @@
     class_ref,
     ins,
     by1,
-    bx1,
     by2,
     bx2,
     by3,
@@ -232,6 +231,10 @@
     rr,
     cs,
     cr,
+    os,
+    orr,
+    gs,
+    gr,
 ):
     loads = [
         pltpu.make_async_copy(src, dst, ins.at[i])
@@ -255,18 +258,19 @@
     def greet(tx, ty):
         pl.semaphore_signal(barrier, inc=1, device_id=(tx, ty), device_id_type=pl.DeviceIdType.MESH)
 
-    for i in range(1, ngx):
-        greet(lax.rem(gx + i, ngx), gy)
-    for i in range(1, ngy):
-        greet(gx, lax.rem(gy + i, ngy))
-    for dx in (-1, 1):
-        for dy in (-1, 1):
-            pl.when(
-                (gx + dx >= 0) & (gx + dx < ngx) & (gy + dy >= 0) & (gy + dy < ngy)
-            )(functools.partial(greet, gx + dx, gy + dy))
-    beside_x = jnp.where(gx > 0, 1, 0) + jnp.where(gx < ngx - 1, 1, 0)
-    beside_y = jnp.where(gy > 0, 1, 0) + jnp.where(gy < ngy - 1, 1, 0)
-    greeted = ngx + ngy - 2 + beside_x * beside_y
+    def everyone(visit):
+        if count <= 64:
+            for i in range(1, count):
+                visit(i, lax.rem(gx + i // ngy, ngx), lax.rem(gy + i % ngy, ngy))
+        else:
+
+            def body(i, carry):
+                visit(i, lax.rem(gx + i // ngy, ngx), lax.rem(gy + lax.rem(i, ngy), ngy))
+                return carry
+
+            lax.fori_loop(1, count, body, 0)
+
+    everyone(lambda i, tx, ty: greet(tx, ty))
 
     def remote(src, dst, send, recv, tx, ty):
         return pltpu.make_async_remote_copy(
@@ -320,6 +324,38 @@
                 copy.wait_recv()
 
         return arrive
+
+    def spread_out(i, tx, ty):
+        return remote(by1.at[gx, gy], by1.at[gx, gy], os.at[i], orr.at[i], tx, ty)
+
+    def spread_in(i, tx, ty):
+        fx = lax.rem(gx + ngx - i // ngy, ngx)
+        fy = lax.rem(gy + ngy - (i % ngy if isinstance(i, int) else lax.rem(i, ngy)), ngy)
+        return remote(by1.at[fx, fy], by1.at[fx, fy], os.at[i], orr.at[i], fx, fy)
+
+    def rows_of(d, j):
+        ty = lax.rem(gy + j, ngy)
+        return remote(
+            r2g.at[REACH, gy], r2g.at[REACH - d, gy], gs.at[d + REACH, j], gr.at[d + REACH, j], gx + d, ty
+        )
+
+    def rows_in(d, j):
+        fy = lax.rem(gy + ngy - j, ngy)
+        return remote(
+            r2g.at[REACH, fy], r2g.at[REACH - d, fy], gs.at[d + REACH, j], gr.at[d + REACH, j], gx - d, fy
+        )
+
+    def across(visit, sign):
+        for d in range(-REACH, REACH + 1):
+            def row(d=d):
+                for j in range(ngy):
+                    if (d, j) != (0, 0):
+                        visit(d, j)
+
+            if d == 0:
+                row()
+            else:
+                pl.when((gx + sign * d >= 0) & (gx + sign * d < ngx))(row)
 
     def reduce_start(slot, val, bufy):
         bufy[gy] = val
@@ -371,7 +407,7 @@
             kh[2 + x // 2, 2 + y, rows, :] = jnp.broadcast_to(conduct[x : x + 1, cut], (4, 128))
             xp[0, 1 + x // 2, 1 + y, rows, :] = modes_ref[:, x, cut]
             xp[1, 1 + x // 2, 1 + y, rows, :] = dirs_ref[:, x, cut]
-    pl.semaphore_wait(barrier, greeted)
+    pl.semaphore_wait(barrier, count - 1)
     arrive_k = halo(0, lambda a, b: kh.at[a, b], 2, True)
     arrive_xp = halo(1, lambda a, b: xp.at[:, a, b], 1, False)
 
@@ -422,19 +458,20 @@
     image_x = stencil(m, xp[0], own_coef)
     image_x8 = flat(image_x)
     image_dots = fold_locked(m, dot_split(image_x8, l_high[...], l_low[...], NT))
-    first = reduce_start(0, jnp.where(m.half0, image_dots, mode_dots), by1)
+    by1[gx, gy] = jnp.where(m.half0, image_dots, mode_dots)[:4]
+    everyone(lambda i, tx, ty: spread_out(i, tx, ty).start())
 
     wide = fine_coef(m, kh[...])
     in_grid = kh[1:5, 1:7] > 0
     dinv0 = inverse(wide[0], in_grid)
-    second = reduce_next(0, first, by1, bx1)
     mid = middle_coef(m, wide)
     dinv1 = inverse(mid[0], in_grid)
     own_mid = [c[1:3, 1:5] for c in mid]
     first_c = gather_start(6, ccg, coarse_pack(m, own_mid))
     image_p = stencil(m, xp[1], own_coef)
-    second()
-    sums = total([bx1[j] for j in range(ngx)])
+    everyone(lambda i, tx, ty: spread_in(i, tx, ty).wait_recv())
+    sums = jnp.sum(by1[...].reshape(count, 4, 128), axis=0)
+    sums = jnp.concatenate([sums, sums], axis=0)
 
     f_of = m.sub % 4
     top = jnp.sum(jnp.where(m.lane == nl + f_of, sums, 0.0), axis=1, keepdims=True)
@@ -491,8 +528,9 @@
     arrive_e1 = halo(3, lambda a, b: e1h.at[a, b], 2, True)
     r2 = r1[1:3, 1:5] - middle_stencil(m, e1_near, own_mid)
     r2 = r2[0] + r2[1]
-    r2 = jnp.where(m.par0, r2[0] + r2[1], r2[2] + r2[3])
-    first_r = gather_start(7, r2g, pair_z2(m, r2))
+    r2 = jnp.where(m.half0, r2[0] + r2[1], r2[2] + r2[3])
+    r2g[REACH, gy] = pair_z2(m, r2)[:4]
+    across(lambda d, j: rows_of(d, j).start(), 1)
     arrive_c()
     lines = 2 * ngy
     shift = 4.0 / float(lines * lines)
@@ -524,15 +562,18 @@
         faces[y][4] = jnp.where(z4 < 4, 0.0, zl)
         faces[y][5] = jnp.where(z4 >= NZ - 4, 0.0, zu)
 
-    arrive_r = gather_next(1, first_r, r2g)
     square = []
     for left in (lst[...], al[...]):
         whole = dot_split(left, l_high[...], l_low[...], NT)
         square.append(whole[:64, :64] + whole[64:, 64:])
     first_s = reduce_start(4, jnp.concatenate(square, axis=1), by3)
-    arrive_r()
-
-    source = [r2g[:, y // 2, 4 * (y % 2) : 4 * (y % 2) + 4] for y in range(lines)]
+    across(lambda d, j: rows_in(d, j).wait_recv(), -1)
+
+    source = []
+    for y in range(lines):
+        tile_y = r2g[:, y // 2]
+        other = lanes(tile_y, 64)
+        source.append(jnp.where(m.half0[:4], *((tile_y, other) if y % 2 == 0 else (other, tile_y))))
     held = []
     for y in range(lines):
         right = source[y] if y == 0 else source[y] + faces[y][2] * held[y - 1]
@@ -625,6 +666,8 @@
         [grams[0], jnp.zeros((24, 8), F32), grams[1], jnp.zeros((24, 72), F32)], axis=1
     )
 
+    everyone(lambda i, tx, ty: spread_out(i, tx, ty).wait_send())
+    across(lambda d, j: rows_of(d, j).wait_send(), 1)
     for copy, to in pending:
         if to is None:
             copy.wait_send()
@@ -731,7 +774,7 @@
             pltpu.VMEM((6, 8, 8, 128), F32),
             pltpu.VMEM((6, 8, 8, 128), F32),
             pltpu.VMEM((wide, ngy, 8, 128), F32),
-            pltpu.VMEM((wide, ngy, 8, 128), F32),
+            pltpu.VMEM((wide, ngy, 4, 128), F32),
             pltpu.VMEM((2 * ngy + 2, 3, 4, 128), F32),
             pltpu.VMEM((64, 512), F32),
             pltpu.VMEM((64, 512), F32),
@@ -747,8 +790,7 @@
             pltpu.VMEM(locked.shape, F32),
             pltpu.VMEM(perm_class.shape, jnp.int32),
             dma((4,)),
-            pltpu.VMEM((ngy, 8, 128), F32),
-            pltpu.VMEM((ngx, 8, 128), F32),
+            pltpu.VMEM((ngx, ngy, 4, 128), F32),
             pltpu.VMEM((ngy, 16, 128), F32),
             pltpu.VMEM((ngx, 16, 128), F32),
             pltpu.VMEM((ngy, 64, 128), F32),
@@ -759,6 +801,10 @@
             dma((8, max(ngx, ngy))),
             dma((2, wide)),
             dma((2, wide)),
+            dma((ngx * ngy,)),
+            dma((ngx * ngy,)),
+            dma((wide, ngy)),
+            dma((wide, ngy)),
         ],
         compiler_params=pltpu.CompilerParams(
             collective_id=0, has_side_effects=True, vmem_limit_bytes=limit

time: 46.9 us -> 45 us (0.959)
  Pallas kernels: 45.3 us -> 43.4 us
    pallas_call x1, Pallas kernels: 40.6 us -> 38.7 us  [on_device(): pl.pallas_call(functools.partial(kernel, ngx, ngy), out_shape=(jax.ShapeD...]
where the time goes in v5:
time: 45 us; the launch traced here: 44.7 us
  Pallas kernels  43.4 us (96%)
  between operations  1.29 us (3%)
    pallas_call x1, Pallas kernels, on_device(): pl.pallas_call(functools.partial(kernel, ngx, ngy), out_shape=(jax.ShapeD...  38.7 us
    pallas_call x1, Pallas kernels, on_device(): pl.pallas_call(finish, out_shape=(jax.ShapeDtypeStruct(modes.shape, F32),...  4.72 us

profile of v5, /device:TPU:0, one launch (start us, length us, event | category | flops | bytes accessed | tf_op | source)
XLA Modules:
  0.0 44.7 jit_solution(1829969195849256831)
XLA Ops:
  1.3 38.7 %shard_map.93 = (f32[24,128]{1,0:T(8,128)}, f32[24,1024]{1,0:T(8,128)}, f32[4,60]{1,0:T(4,128)}) custom-call(f32[4,4,512]{2,1,0:T(4,128)} %modes_hbm.1, f32[4,4,512]{2,1,0:T(4,128)} %dirs_hbm.1, f32[60,4,512]{2,1,0:T(4,128)} %locked_hbm.1, s32[4,512]{1,0:T(4,128)} %class_hbm.1, f32[16]{0:T(128)} %table_ref.1, s32[1]{0:T(128)S(6)} %copy.10.count_ref), custom_call_target="tpu_custom_call" | custom-call | tf_op jit(solution)/shard_map/pallas_call | solution.py:762
  40.0 4.7 %shard_map.94 = (f32[4,4,512]{2,1,0:T(4,128)}, f32[4,4,512]{2,1,0:T(4,128)}, f32[4]{0:T(128)}, f32[4,60]{1,0:T(4,128)}) custom-call(f32[24,128]{1,0:T(8,128)} %get-tuple-element.11.sums_hbm, f32[24,1024]{1,0:T(8,128)} %get-tuple-element.12.trial_hbm, f32[4,60]{1,0:T(4,128)} %get-tuple-element.13.corr_hbm), custom_call_target="tpu_custom_call" | custom-call | tf_op jit(solution)/shard_map/pallas_call | solution.py:813

commit v6 on v5

--- a/solution.py
+++ b/solution.py
@@ -601,6 +601,7 @@
     near = e2s[pl.ds(2 * gy, 4)]
     near = jnp.concatenate([near, near], axis=2)
 
+    second_s = reduce_next(4, first_s, by3, bx3)
     arrive_e1()
     e1_wide = e1h[...]
     e1_wide = jnp.stack(
@@ -631,7 +632,6 @@
     own = jnp.where(m.par0, among[0], among[1])
     own = own + lanes(own, -4)
     first = reduce_start(2, jnp.concatenate([cross, own], axis=0), by2)
-    second_s = reduce_next(4, first_s, by3, bx3)
     late = reduce_end(2, first, by2, bx2) / cells
     cross, own = late[:8], late[8:]
     corr = jnp.where(in_use & m.half0 & m.par0, cross, 0.0)

time: 45 us -> 46.2 us (1.027)
  Pallas kernels: 43.4 us -> 44.6 us
    pallas_call x1, Pallas kernels: 38.7 us -> 39.9 us  [on_device(): pl.pallas_call(functools.partial(kernel, ngx, ngy), out_shape=(jax.ShapeD...]
where the time goes in v6:
time: 46.2 us; the launch traced here: 45.9 us
  Pallas kernels  44.6 us (97%)
  between operations  1.29 us (3%)
    pallas_call x1, Pallas kernels, on_device(): pl.pallas_call(functools.partial(kernel, ngx, ngy), out_shape=(jax.ShapeD...  39.9 us
    pallas_call x1, Pallas kernels, on_device(): pl.pallas_call(finish, out_shape=(jax.ShapeDtypeStruct(modes.shape, F32),...  4.72 us

profile of v6, /device:TPU:0, one launch (start us, length us, event | category | flops | bytes accessed | tf_op | source)
XLA Modules:
  0.0 45.9 jit_solution(3539137002152957096)
XLA Ops:
  1.3 39.9 %shard_map.93 = (f32[24,128]{1,0:T(8,128)}, f32[24,1024]{1,0:T(8,128)}, f32[4,60]{1,0:T(4,128)}) custom-call(f32[4,4,512]{2,1,0:T(4,128)} %modes_hbm.1, f32[4,4,512]{2,1,0:T(4,128)} %dirs_hbm.1, f32[60,4,512]{2,1,0:T(4,128)} %locked_hbm.1, s32[4,512]{1,0:T(4,128)} %class_hbm.1, f32[16]{0:T(128)} %table_ref.1, s32[1]{0:T(128)S(6)} %copy.10.count_ref), custom_call_target="tpu_custom_call" | custom-call | tf_op jit(solution)/shard_map/pallas_call | solution.py:762
  41.2 4.7 %shard_map.94 = (f32[4,4,512]{2,1,0:T(4,128)}, f32[4,4,512]{2,1,0:T(4,128)}, f32[4]{0:T(128)}, f32[4,60]{1,0:T(4,128)}) custom-call(f32[24,128]{1,0:T(8,128)} %get-tuple-element.11.sums_hbm, f32[24,1024]{1,0:T(8,128)} %get-tuple-element.12.trial_hbm, f32[4,60]{1,0:T(4,128)} %get-tuple-element.13.corr_hbm), custom_call_target="tpu_custom_call" | custom-call | tf_op jit(solution)/shard_map/pallas_call | solution.py:813
